TPU v7x, 32 devices: a whole 2x2x4 slice. The times are simulated.
32 devices in a mesh: tp: 16 (over z, y, core), ep: 2 (over x).
Axes of the slice: x: 2, y: 2, z: 4, core: 2. Of those that a mesh axis runs over, the one named last changes fastest.
Arguments:
- residual: bfloat16 [2, 7168, 256], P('ep', 'tp')
- out_grad: bfloat16 [2, 7168, 256], P('ep', 'tp'), may hold values from -6 to 6
- norm_gain: float32 [7168], P('tp'), may hold values from 0.25 to 1.75
- context: bfloat16 [2, 16384, 256], P('ep', 'tp'), may hold values from -0.625 to 0.625
- w_out: bfloat16 [7168, 16384], P('ep', 'tp'), may hold values from -0.046875 to 0.046875
- w_gate: bfloat16 [2, 7168, 2048], P('ep', 'tp'), may hold values from -0.0625 to 0.0625
- w_up: bfloat16 [2, 7168, 2048], P('ep', 'tp'), may hold values from -0.0625 to 0.0625
- w_down: bfloat16 [2, 7168, 2048], P('ep', 'tp'), may hold values from -0.125 to 0.125
- slot_token: int32 [2, 2, 8], P('ep'), may hold values from 0 to 255, as said below
- slot_count: int32 [2, 2], P('ep'), may hold values from 1 to 8, as said below
- slot_gate: float32 [2, 2, 8], P('ep'), may hold values from 0.25 to 2.5
Outputs:
- resid_grad: bfloat16 [2, 7168, 256], P('ep', 'tp')
- context_grad: bfloat16 [2, 16384, 256], P('ep', 'tp')
- w_out_grad: bfloat16 [7168, 16384], P('ep', 'tp')
- gate_grad: bfloat16 [2, 7168, 2048], P('ep', 'tp')
- up_grad: bfloat16 [2, 7168, 2048], P('ep', 'tp')
- down_grad: bfloat16 [2, 7168, 2048], P('ep', 'tp')
Inputs may be any that keep to these rules, and one draw needn't show every extreme that they name: `slot_token`: within one group and expert the 8 token positions are distinct; slots at or beyond slot_count are unused. `slot_count`: in every draw one expert has 8 tokens from every group.
All inputs are finite; a program needn't handle non-finite values.
Results may differ from a plain program's by a relative error of at most 0.014.
Values may be sent and summed in bfloat16 or wider, within the bound.
No kernel may reach another device: no remote copies, remote signals or barrier semaphores. Data moves between devices by JAX's collectives and lax.ppermute only.
A program may use at most 128 MiB of HBM per device.

v0:
```python
import jax
import jax.numpy as jnp
from jax import lax
from jax.sharding import PartitionSpec as P

norm_eps = 1e-06


def contract_rows(left, right):
    return lax.dot_general(
        left, right, (((0,), (0,)), ((), ())), preferred_element_type=jnp.float32
    )


def contract_cols(left, right):
    return lax.dot_general(
        left, right, (((1,), (1,)), ((), ())), preferred_element_type=jnp.float32
    )


def activate(pre_gate, pre_up, hid_grad):
    sigmoid_gate = jax.nn.sigmoid(pre_gate)
    silu_gate = pre_gate * sigmoid_gate
    hidden = (silu_gate * pre_up).astype(jnp.bfloat16)
    d_gate = (hid_grad * pre_up * sigmoid_gate * (1.0 + pre_gate * (1.0 - sigmoid_gate))).astype(
        jnp.bfloat16
    )
    d_up = (hid_grad * silu_gate).astype(jnp.bfloat16)
    return (hidden, d_gate, d_up)


def shards(
    residual,
    out_grad,
    norm_gain,
    context,
    w_out,
    w_gate,
    w_up,
    w_down,
    slot_token,
    slot_count,
    slot_gate,
):
    tp_count = lax.axis_size("tp")
    stream = residual[0].astype(jnp.float32)
    grad_in = out_grad[0].astype(jnp.float32)
    feat_share, group_rows = stream.shape
    features = feat_share * tp_count
    square = lax.psum(jnp.sum(stream * stream, axis=0), "tp")
    inv_rms = lax.rsqrt(square / features + norm_eps)[None, :]
    normed = stream * inv_rms
    gain_col = norm_gain[:, None]
    inputs = (normed * gain_col).astype(jnp.bfloat16)
    slot_table = slot_token[0]
    capacity = slot_table.shape[1]
    live_mask = jnp.arange(capacity)[None, :] < slot_count[0][:, None]
    one_hot = (
        (slot_table[:, :, None] == jnp.arange(group_rows)[None, None, :]) & live_mask[:, :, None]
    ).astype(jnp.bfloat16)
    send_x = jnp.einsum("dt,ect->edc", inputs, one_hot, preferred_element_type=jnp.float32).astype(
        jnp.bfloat16
    )
    go_rows = jnp.einsum("dt,ect->edc", out_grad[0], one_hot, preferred_element_type=jnp.float32)
    send_go = (slot_gate[0][:, None, :] * go_rows).astype(jnp.bfloat16)
    recv_x, recv_go = (
        lax.all_to_all(send_x, "ep", split_axis=0, concat_axis=2, tiled=True),
        lax.all_to_all(send_go, "ep", split_axis=0, concat_axis=2, tiled=True),
    )
    rows_x = recv_x[0]
    rows_go = recv_go[0]
    gate_w = w_gate[0]
    up_w = w_up[0]
    down_w = w_down[0]
    gate_part = contract_rows(rows_x, gate_w)
    up_part = contract_rows(rows_x, up_w)
    hid_part = contract_rows(rows_go, down_w)
    pre_gate, pre_up, hid_grad = lax.psum((gate_part, up_part, hid_part), "tp")
    hidden, d_gate, d_up = activate(pre_gate, pre_up, hid_grad)
    down_grad = jnp.dot(rows_go, hidden, preferred_element_type=jnp.float32).astype(jnp.bfloat16)[
        None
    ]
    gate_grad = jnp.dot(rows_x, d_gate, preferred_element_type=jnp.float32).astype(jnp.bfloat16)[
        None
    ]
    up_grad = jnp.dot(rows_x, d_up, preferred_element_type=jnp.float32).astype(jnp.bfloat16)[None]
    slot_back = (contract_cols(gate_w, d_gate) + contract_cols(up_w, d_up)).astype(jnp.bfloat16)
    returned = lax.all_to_all(slot_back[None], "ep", split_axis=2, concat_axis=0, tiled=True)
    in_grad = jnp.einsum(
        "edc,ect->dt", returned, one_hot, preferred_element_type=jnp.float32
    ).astype(jnp.bfloat16)
    scaled = in_grad.astype(jnp.float32) * gain_col
    dots = lax.psum(jnp.sum(scaled * normed, axis=0), "tp")
    resid = (grad_in + inv_rms * (scaled - normed * (dots / features)[None, :])).astype(
        jnp.bfloat16
    )
    full_grad = lax.all_gather(resid, "tp", axis=0, tiled=True)
    grad_block = lax.all_to_all(full_grad, "ep", split_axis=0, concat_axis=1, tiled=True)
    ctx_local = context[0]
    ctx_all = lax.all_gather(ctx_local, "ep", axis=1, tiled=True)
    weight_sum = contract_cols(grad_block, ctx_all)
    ctx_total = contract_rows(lax.all_gather(w_out, "ep", axis=0, tiled=True), full_grad)
    return (
        resid[None],
        ctx_total.astype(jnp.bfloat16)[None],
        weight_sum.astype(jnp.bfloat16),
        gate_grad,
        up_grad,
        down_grad,
    )


def solution(mesh):
    return jax.shard_map(
        shards,
        mesh=mesh,
        in_specs=(
            P("ep", "tp", None),
            P("ep", "tp", None),
            P("tp"),
            P("ep", "tp", None),
            P("ep", "tp"),
            P("ep", "tp", None),
            P("ep", "tp", None),
            P("ep", "tp", None),
            P("ep", None, None),
            P("ep", None),
            P("ep", None, None),
        ),
        out_specs=(
            P("ep", "tp", None),
            P("ep", "tp", None),
            P("ep", "tp"),
            P("ep", "tp", None),
            P("ep", "tp", None),
            P("ep", "tp", None),
        ),
        check_vma=False,
    )
```

profile of v0, /device:TPU:0, one launch (start us, length us, event | category | flops | bytes accessed | tf_op | source)
XLA Modules:
  0.0 471.2 jit_solution(9592606120190340347)
XLA Ops:
  7.2 0.0 copy-start
  7.2 1.2 fusion.39
  8.3 34.9 %psum.35 = f32[256]{0:T(256)S(1)} all-reduce(f32[256]{0:T(256)S(1)} %fusion.39), channel_id=1, replica_groups=mesh['tp'=16,'ep'=2] {'tp'}, use_global_device_ids=true, to_apply=%region_1.0 | all-reduce | flops 256 | bytes 2048 | tf_op jit(solution)/shard_map/psum | solution.py:50
  43.3 0.7 iota_compare_fusion.1
  44.0 1.8 fusion.24
  45.8 3.2 all-to-all-start.1
  49.0 1.7 fusion.28
  50.8 2.1 all-to-all-done.1
  52.9 3.2 all-to-all-start
  56.1 0.0 all-reduce.3.cloned.1.call-start
  56.2 0.0 copy-done
  56.2 0.0 copy-start.1
  56.2 1.0 fusion.5
  57.2 0.5 copy-done.1
  57.7 1.0 fusion.9
  58.8 1.2 all-to-all-done
  60.0 2.5 fusion.11
  62.5 0.0 all-reduce.3.cloned.1.call-update
  62.5 0.0 all-gather.5.cloned.1.call-start
  62.6 87.7 %all-reduce.3.cloned.1.call-done = (f32[16,2048]{1,0:T(8,128)}, f32[16,2048]{1,0:T(8,128)}, f32[16,2048]{1,0:T(8,128)}) async-done(((f32[16,2048]{1,0:T(8,128)}, f32[16,2048]{1,0:T(8,128)}, f32[16,2048]{1,0:T(8,128)}), (f32[16,2048]{1,0:T(8,128)}, f32[16,2048]{1,0:T(8,128)}, f32[16,2048]{1,0:T(8,128)})) %all-reduce.3.cloned.1.call-update) | async-done | bytes 393232 | tf_op jit(solution)/shard_map/psum | solution.py:78
  150.2 0.0 copy-start.2
  150.2 1.2 multiply_convert_fusion.1
  151.5 0.0 copy-start.3
  151.5 0.0 copy-start.7
  151.5 0.0 copy-start.8
  151.5 0.6 fusion.3
  152.1 0.0 copy-start.6
  152.1 0.0 copy-done.2
  152.1 0.6 fusion.25
  152.8 0.5 broadcast.36
  153.3 0.7 reduce
  154.0 0.1 reshape.53
  154.1 6.4 %all_to_all.67 = bf16[2,2,1792]{2,1,0:T(2,128)(2,1)S(1)} all-to-all(bf16[2,2,1792]{2,1,0:T(2,128)(2,1)S(1)} %reshape.53), channel_id=1, replica_groups=mesh['tp'=16,'ep'=2] {'ep'}, dimensions={0} | all-to-all | bytes 28672 | tf_op jit(solution)/shard_map/all_to_all | solution.py:88
  160.5 0.1 reshape.54
  160.6 0.0 copy-done.3
  160.6 0.0 copy-done.7
  160.6 0.0 copy-done.8
  160.6 0.3 fusion.34
  160.9 29.5 %psum.39 = f32[256]{0:T(256)S(1)} all-reduce(f32[256]{0:T(256)S(1)} %get-tuple-element.35), channel_id=1, replica_groups=mesh['tp'=16,'ep'=2] {'tp'}, use_global_device_ids=true, to_apply=%region_6.0 | all-reduce | flops 256 | bytes 2048 | tf_op jit(solution)/shard_map/psum | solution.py:93
  190.4 0.0 copy-done.6
  190.4 0.8 fusion.38
  191.2 0.0 all-gather.5.cloned.1.call-update
  191.2 0.0 all-gather.9.cloned.1.call-start
  191.3 0.7 all-gather.9.cloned.1.call-update
  192.0 0.0 all-gather.7.cloned.1.call-start
  192.0 0.5 all-gather.7.cloned.1.call-update
  192.6 42.2 %all-gather.5.cloned.1.call-done = bf16[7168,256]{1,0:T(8,128)(2,1)} async-done(((bf16[448,256]{1,0:T(8,128)(2,1)}), bf16[7168,256]{1,0:T(8,128)(2,1)}) %all-gather.5.cloned.1.call-update) | async-done | bytes 3670032 | tf_op jit(solution)/shard_map/all_gather | solution.py:97
  234.8 5.9 %copy.24 = bf16[2,3584,256]{1,2,0:T(8,128)(2,1)} copy(bf16[2,3584,256]{2,1,0:T(8,128)(2,1)} %bitcast.115) | data formatting | bytes 7340032 | tf_op jit(solution)/shard_map/all_to_all | solution.py:98
  240.7 5.6 %all-to-all-start.3 = ((bf16[2,3584,256]{1,2,0:T(8,128)(2,1)}), bf16[2,3584,256]{1,2,0:T(8,128)(2,1)}, u32[]{:S(2)}, u32[]{:S(2)}) async-start(bf16[2,3584,256]{1,2,0:T(8,128)(2,1)} %copy.24), calls=%async_computation.3 | async-start | bytes 7340032 | tf_op jit(solution)/shard_map/all_to_all | solution.py:98
  246.3 0.0 copy-start.4
  246.3 0.0 copy-start.5
  246.4 1.9 fusion
  248.2 1.9 fusion.1
  250.1 0.0 copy-done.4
  250.1 0.0 copy-done.5
  250.1 1.9 fusion.2
  252.0 12.0 %all-gather.9.cloned.1.call-done = bf16[1,1024,512]{2,1,0:T(8,128)(2,1)} async-done(((bf16[1,1024,256]{2,1,0:T(8,128)(2,1)}), bf16[1,1024,512]{2,1,0:T(8,128)(2,1)}) %all-gather.9.cloned.1.call-update) | async-done | bytes 1048592 | tf_op jit(solution)/shard_map/all_gather | solution.py:100
  264.1 42.3 %all-to-all-done.3 = bf16[2,3584,256]{1,2,0:T(8,128)(2,1)} async-done(((bf16[2,3584,256]{1,2,0:T(8,128)(2,1)}), bf16[2,3584,256]{1,2,0:T(8,128)(2,1)}, u32[]{:S(2)}, u32[]{:S(2)}) %all-to-all-start.3) | async-done | bytes 3670048 | tf_op jit(solution)/shard_map/all_to_all | solution.py:98
  306.3 9.4 %convolution_convert_fusion = bf16[3584,1024]{1,0:T(8,128)(2,1)} fusion(bf16[3584,512]{0,1:T(8,128)(2,1)} %bitcast.31, bf16[1,1024,512]{2,1,0:T(8,128)(2,1)} %all-gather.9.cloned.1.call-done), kind=kOutput, calls=%fused_computation | convolution fusion | flops 3761766400 | bytes 12058624 | tf_op jit(solution)/shard_map/dot_general | solution.py:16
  315.7 137.6 %all-gather.7.cloned.1.call-done = bf16[7168,1024]{1,0:T(8,128)(2,1)} async-done(((bf16[3584,1024]{1,0:T(8,128)(2,1)}), bf16[7168,1024]{1,0:T(8,128)(2,1)}) %all-gather.7.cloned.1.call-update) | async-done | bytes 14680080 | tf_op jit(solution)/shard_map/all_gather | solution.py:102
  453.4 10.3 %fusion.13 = bf16[1,1024,256]{1,2,0:T(8,128)(2,1)S(1)} fusion(bf16[7168,256]{1,0:T(8,128)(2,1)} %all-gather.5.cloned.1.call-done, bf16[7168,1024]{1,0:T(8,128)(2,1)} %all-gather.7.cloned.1.call-done), kind=kOutput, calls=%fused_computation.18 | convolution fusion | flops 3758358528 | bytes 18874368 | tf_op jit(solution)/shard_map/dot_general | solution.py:10
  463.6 1.0 copy.25
  (3 shorter events, 0.1 us)
Async XLA Ops:
  7.2 49.0 %copy-start = (bf16[1,448,2048]{2,1,0:T(8,128)(2,1)S(1)}, bf16[1,448,2048]{2,1,0:T(8,128)(2,1)}, u32[]{:S(2)}) copy-start(bf16[1,448,2048]{2,1,0:T(8,128)(2,1)} %param.16) | copy-start | bytes 5505028
  45.8 7.1 %all-to-all-start.1 = ((bf16[2,448,8]{1,2,0:T(8,128)(2,1)}), bf16[2,448,8]{1,2,0:T(8,128)(2,1)S(1)}, u32[]{:S(2)}, u32[]{:S(2)}) async-start(bf16[2,448,8]{1,2,0:T(8,128)(2,1)} %fusion.24), calls=%async_computation.1 | async-start | bytes 32768 | tf_op jit(solution)/shard_map/all_to_all | solution.py:67
  52.9 7.1 %all-to-all-start = ((bf16[2,448,8]{1,2,0:T(8,128)(2,1)}), bf16[2,448,8]{1,2,0:T(8,128)(2,1)S(1)}, u32[]{:S(2)}, u32[]{:S(2)}) async-start(bf16[2,448,8]{1,2,0:T(8,128)(2,1)} %fusion.28), calls=%async_computation | async-start | bytes 32768 | tf_op jit(solution)/shard_map/all_to_all | solution.py:68
  56.1 94.1 %all-reduce.3.cloned.1.call-start = ((), (), s32[]{:S(2)}) async-start(), calls=%async_computation.7 | async-start | bytes 786432 | tf_op jit(solution)/shard_map/psum | solution.py:78
  56.2 1.5 copy-start.1
  62.5 172.3 %all-gather.5.cloned.1.call-start = ((), (), s32[]{:S(2)}) async-start(), calls=%async_computation.4 | async-start | bytes 3899392 | tf_op jit(solution)/shard_map/all_gather | solution.py:97
  150.2 1.9 copy-start.2
  151.5 9.1 %copy-start.3 = (bf16[1,448,256]{2,1,0:T(8,128)(2,1)S(1)}, bf16[1,448,256]{2,1,0:T(8,128)(2,1)}, u32[]{:S(2)}) copy-start(bf16[1,448,256]{2,1,0:T(8,128)(2,1)} %param.11) | copy-start | bytes 688132
  151.5 9.1 %copy-start.7 = (f32[448]{0:T(512)S(1)}, f32[448]{0:T(512)}, u32[]{:S(2)}) copy-start(f32[448]{0:T(512)} %param.13) | copy-start | bytes 5380
  151.5 9.1 %copy-start.8 = (s32[1,2,8]{2,1,0:T(2,128)S(1)}, s32[1,2,8]{2,1,0:T(2,128)}, u32[]{:S(2)}) copy-start(s32[1,2,8]{2,1,0:T(2,128)} %param.19) | copy-start | bytes 196
  152.1 38.3 %copy-start.6 = (bf16[1,448,256]{2,1,0:T(8,128)(2,1)S(1)}, bf16[1,448,256]{2,1,0:T(8,128)(2,1)}, u32[]{:S(2)}) copy-start(bf16[1,448,256]{2,1,0:T(8,128)(2,1)} %param.12) | copy-start | bytes 688132
  191.2 72.8 %all-gather.9.cloned.1.call-start = ((), (), s32[]{:S(2)}) async-start(), calls=%async_computation.6 | async-start | bytes 1572864 | tf_op jit(solution)/shard_map/all_gather | solution.py:100
  192.0 261.4 %all-gather.7.cloned.1.call-start = ((), (), s32[]{:S(2)}) async-start(), calls=%async_computation.5 | async-start | bytes 22020096 | tf_op jit(solution)/shard_map/all_gather | solution.py:102
  240.7 65.6 %all-to-all-start.3 = ((bf16[2,3584,256]{1,2,0:T(8,128)(2,1)}), bf16[2,3584,256]{1,2,0:T(8,128)(2,1)}, u32[]{:S(2)}, u32[]{:S(2)}) async-start(bf16[2,3584,256]{1,2,0:T(8,128)(2,1)} %copy.24), calls=%async_computation.3 | async-start | bytes 7340032 | tf_op jit(solution)/shard_map/all_to_all | solution.py:98
  246.3 3.8 copy-start.4
  246.3 3.8 copy-start.5
Sparse Core Ops, SparseCore 0:
  62.6 87.5 all-reduce.2
  191.4 43.3 all-gather.4
  236.4 27.6 all-gather.8
  265.6 187.7 all-gather.6
where the time goes:
time: 472 us; the launch traced here: 471 us
  waiting for transfers between devices  326 us (69%)
  blocking collectives  70.8 us (15%)
  matrix products  34.9 us (7%)
  between operations  13.9 us (3%)
  starting transfers between devices  12.2 us (3%)
  local copies, waits for them, and re-layouts  8.26 us (2%)
    all_gather x1, waiting for transfers between devices, shards(): lax.all_gather(w_out, 'ep', axis=0, tiled=True)  138 us
    psum x1, waiting for transfers between devices, shards(): pre_gate, pre_up, hid_grad = lax.psum((gate_part, up_part, hid_part), 'tp')  87.7 us
    all_to_all x1, waiting for transfers between devices, shards(): lax.all_to_all(full_grad, 'ep', split_axis=0, concat_axis=1, tiled=True)  42.3 us
    all_gather x1, waiting for transfers between devices, shards(): full_grad = lax.all_gather(resid, 'tp', axis=0, tiled=True)  42.2 us
    psum x1, blocking collectives, shards(): square = lax.psum(jnp.sum(stream * stream, axis=0), 'tp')  34.9 us
    psum x1, blocking collectives, shards(): dots = lax.psum(jnp.sum(scaled * normed, axis=0), 'tp')  29.5 us
    dot_general x4, matrix products, contract_rows(): lax.dot_general(left, right, (((0,), (0,)), ((), ())), preferred_element_...  14.8 us
    all_gather x1, waiting for transfers between devices, shards(): ctx_all = lax.all_gather(ctx_local, 'ep', axis=1, tiled=True)  12 us
  transfers between devices with their start and end apart: 7, of which 7 were waited for; matrix products, arithmetic and copies ran while one was open for 5% of the time, Pallas kernels for 0%

commit v1 on v0

v1 whole, which is shorter than its diff:
```python
import functools

import jax
import jax.numpy as jnp
from jax import lax
from jax.experimental import pallas as pl
from jax.experimental.pallas import tpu as pltpu
from jax.sharding import PartitionSpec as P

norm_eps = 1e-06
BF = jnp.bfloat16
F32 = jnp.float32
MIB = 1024 * 1024


def mm(left, right):
    return jnp.dot(left, right, preferred_element_type=F32)


def contract_rows(left, right):
    return lax.dot_general(left, right, (((0,), (0,)), ((), ())), preferred_element_type=F32)


def contract_cols(left, right):
    return lax.dot_general(left, right, (((1,), (1,)), ((), ())), preferred_element_type=F32)


def split_two(value):
    high = value.astype(BF).astype(F32)
    rest = jnp.where(jnp.abs(value) < jnp.inf, value - high, 0.0)
    return high, rest


def lane_ids(shape):
    return lax.broadcasted_iota(jnp.int32, shape, len(shape) - 1)


def row_ids(shape):
    return lax.broadcasted_iota(jnp.int32, shape, len(shape) - 2)


def two_lanes(value, shape):
    high, rest = split_two(value)
    lane = lane_ids(shape)
    return jnp.where(lane == 0, high, jnp.where(lane == 1, rest, 0.0))


def call(kernel, outs, operands, in_specs, out_specs, grid=None, scratch=(), flops=0, limit=52):
    size = 0
    for leaf in list(outs) + list(operands):
        count = 1
        for dim in leaf.shape:
            count *= dim
        size += count * leaf.dtype.itemsize
    extra = {} if grid is None else {"grid": grid}
    return pl.pallas_call(
        kernel,
        out_shape=tuple(outs),
        in_specs=in_specs,
        out_specs=tuple(out_specs),
        scratch_shapes=list(scratch),
        compiler_params=pltpu.CompilerParams(vmem_limit_bytes=limit * MIB),
        cost_estimate=pl.CostEstimate(flops=flops, bytes_accessed=size, transcendentals=0),
        **extra,
    )(*operands)


VMEM = pl.BlockSpec(memory_space=pltpu.VMEM)
HBM = pl.BlockSpec(memory_space=pltpu.HBM)


def shape_of(shape, dtype=BF):
    return jax.ShapeDtypeStruct(shape, dtype)


def one_hot(pos, tokens):
    hit = pos.astype(jnp.int32) == lane_ids((pos.shape[0], tokens))
    return jnp.where(hit, 1.0, 0.0).astype(BF)


def pick_kernel(token_ref, count_ref, gate_ref, resid_ref, out_ref, *sends):
    experts, capacity = token_ref.shape[1:]
    feat, tokens = resid_ref.shape[1:]
    lanes = sends[0].shape[1]
    slots = experts * capacity
    ep = lax.axis_index("ep")

    def column(ref):
        rows = []
        for s in range(experts):
            e = lax.rem(ep + s, experts)
            rows.append(jnp.broadcast_to(ref[0, pl.ds(e, 1), :], (capacity, capacity)))
        rows = jnp.concatenate(rows, axis=0)
        shape = (slots, capacity)
        mine = lane_ids(shape) == lax.rem(row_ids(shape), capacity)
        return jnp.sum(jnp.where(mine, rows.astype(F32), 0.0), axis=1, keepdims=True)

    counts = jnp.sum(
        jnp.where(
            lane_ids((slots, experts))
            == lax.rem(ep + row_ids((slots, experts)) // capacity, experts),
            jnp.broadcast_to(count_ref[...], (slots, experts)),
            0,
        ).astype(F32),
        axis=1,
        keepdims=True,
    )
    order = lax.rem(row_ids((slots, 1)), capacity).astype(F32)
    pos = jnp.where(order < counts, column(token_ref), -1.0)
    hot = one_hot(pos, tokens)
    picked = contract_cols(hot, resid_ref[0])
    grads = column(gate_ref) * contract_cols(hot, out_ref[0])
    for s in range(experts):
        rows = slice(s * capacity, (s + 1) * capacity)
        sends[s][:, :feat] = jnp.concatenate([picked[rows], grads[rows]], axis=0).astype(BF)
        tail = jnp.concatenate([pos[rows], pos[rows]], axis=0)
        sends[s][:, feat:] = jnp.broadcast_to(tail, (2 * capacity, lanes - feat)).astype(BF)


def rows_of(blocks, feat):
    blocks = [b[...].astype(F32) for b in blocks]
    capacity = blocks[0].shape[0] // 2
    x = jnp.concatenate([b[:capacity, :feat] for b in blocks], axis=0)
    go = jnp.concatenate([b[capacity:, :feat] for b in blocks], axis=0)
    pos = jnp.concatenate([b[:capacity, feat : feat + 1] for b in blocks], axis=0)
    return x, go, pos


def fetch(sources, buffer, sems, steps):
    tile = buffer.shape[2] // steps
    copies = []
    for i in range(steps):
        part = slice(i * tile, (i + 1) * tile)
        row = []
        for n, source in enumerate(sources):
            row.append(
                pltpu.make_async_copy(
                    source.at[0, :, part], buffer.at[n, :, part], sems.at[n, i]
                )
            )
            row[-1].start()
        copies.append(row)
    return copies


def parts_kernel(features, groups, steps, *refs):
    got = refs[:groups]
    gain_ref, gate_ref, up_ref, down_ref, sums_ref, buffer, sems = refs[groups:]
    copies = fetch((gate_ref, up_ref, down_ref), buffer, sems, steps)
    feat = buffer.shape[1]
    low, high, _, lanes = sums_ref.shape
    count = low * high
    unit = buffer.shape[2] // count
    chunk = count // steps
    tile = unit * chunk
    x, go, _ = rows_of(got, feat)
    gained = (x * gain_ref[:1]).astype(BF)
    go = go.astype(BF)
    square = jnp.sum(x * x, axis=1, keepdims=True) / features
    tail = two_lanes(square, (x.shape[0], lanes - 3 * unit)).astype(BF)
    for i in range(steps):
        for n, rows in enumerate((gained, gained, go)):
            copies[i][n].wait()
            part = mm(rows, buffer[n, :, i * tile : (i + 1) * tile]).astype(BF)
            for k in range(chunk):
                u = i * chunk + k
                place = slice(n * unit, (n + 1) * unit)
                sums_ref[u % low, u // low, :, place] = part[:, k * unit : (k + 1) * unit]
        for k in range(chunk):
            u = i * chunk + k
            sums_ref[u % low, u // low, :, 3 * unit :] = tail


def add_kernel(parts_ref, total_ref):
    total = parts_ref[0].astype(F32)
    for k in range(1, parts_ref.shape[0]):
        total = total + parts_ref[k].astype(F32)
    total_ref[...] = total.astype(BF)


def activate(sums, unit):
    square = sums[:, 3 * unit : 3 * unit + 1] + sums[:, 3 * unit + 1 : 3 * unit + 2]
    inv_rms = lax.rsqrt(square + norm_eps)
    pre_gate = jnp.where(inv_rms > 0, sums[:, :unit] * inv_rms, 0.0)
    pre_up = jnp.where(inv_rms > 0, sums[:, unit : 2 * unit] * inv_rms, 0.0)
    hid_grad = sums[:, 2 * unit : 3 * unit]
    sigmoid_gate = 1.0 / (1.0 + jnp.exp(-pre_gate))
    silu_gate = pre_gate * sigmoid_gate
    hidden = (silu_gate * pre_up).astype(BF)
    d_gate = (hid_grad * pre_up * sigmoid_gate * (1.0 + pre_gate * (1.0 - sigmoid_gate))).astype(BF)
    d_up = (hid_grad * silu_gate).astype(BF)
    dots = jnp.sum(
        d_gate.astype(F32) * pre_gate + d_up.astype(F32) * pre_up, axis=1, keepdims=True
    )
    tail = two_lanes(dots, (sums.shape[0], sums.shape[1] - 3 * unit)).astype(BF)
    return inv_rms, jnp.concatenate([hidden, d_gate, d_up, tail], axis=1)


def act_kernel(unit, sums_ref, inv_ref, acts_ref):
    total = sums_ref[0].astype(F32)
    for k in range(1, sums_ref.shape[0]):
        total = total + sums_ref[k].astype(F32)
    inv_rms, acts = activate(total, unit)
    inv_ref[...] = jnp.broadcast_to(inv_rms, inv_ref.shape)
    for k in range(acts_ref.shape[0]):
        acts_ref[k] = acts


def delta_kernel(features, unit, groups, steps, *refs):
    got = refs[:groups]
    acts_ref, gain_ref, inv_ref, gate_ref, up_ref = refs[groups : groups + 5]
    hidden_ref, dgate_ref, dup_ref, slot_ref, go_ref, delta_ref = refs[groups + 5 : groups + 11]
    backs = refs[groups + 11 : 2 * groups + 11]
    buffer, sems = refs[2 * groups + 11 :]
    copies = fetch((gate_ref, up_ref), buffer, sems, steps)
    feat = buffer.shape[1]
    low, high = acts_ref.shape[:2]
    count = low * high
    chunk = count // steps
    tile = unit * chunk
    x, go, pos = rows_of(got, feat)
    inv_rms = inv_ref[:, :1]
    normed = x * inv_rms
    slot_ref[...] = (normed * gain_ref[:1]).astype(BF)
    go_ref[...] = go.astype(BF)
    dots = acts_ref[0, 0, :, 3 * unit : 3 * unit + 128].astype(F32)
    for u in range(1, count):
        dots = dots + acts_ref[u % low, u // low, :, 3 * unit : 3 * unit + 128].astype(F32)
    dots = (dots[:, :1] + dots[:, 1:2]) / features
    total = jnp.zeros((x.shape[0], feat), F32)
    for i in range(steps):
        part = slice(i * tile, (i + 1) * tile)
        for n, ref in enumerate((hidden_ref, dgate_ref, dup_ref)):
            place = slice(n * unit, (n + 1) * unit)
            value = jnp.concatenate(
                [acts_ref[u % low, u // low, :, place] for u in range(i * chunk, (i + 1) * chunk)],
                axis=1,
            )
            ref[:, part] = value
            if n > 0:
                copies[i][n - 1].wait()
                total = total + contract_cols(value, buffer[n - 1, :, part])
    change = inv_rms * (total * gain_ref[:1] - normed * dots)
    tail = jnp.broadcast_to(pos, (pos.shape[0], delta_ref.shape[1] - feat))
    delta_ref[:, :feat] = change.astype(BF)
    delta_ref[:, feat:] = tail.astype(BF)
    capacity = backs[0].shape[0]
    for s in range(groups):
        rows = slice(s * capacity, (s + 1) * capacity)
        backs[s][:, :feat] = change[rows]
        backs[s][:, feat:] = tail[rows]


def grads_kernel(slot_ref, go_ref, hidden_ref, dgate_ref, dup_ref, gate_out, up_out, down_out):
    gate_out[0] = contract_rows(slot_ref[...], dgate_ref[...]).astype(BF)
    up_out[0] = contract_rows(slot_ref[...], dup_ref[...]).astype(BF)
    down_out[0] = contract_rows(go_ref[...], hidden_ref[...]).astype(BF)


def back_rows(backs, feat):
    rows = jnp.concatenate([b[...] for b in backs], axis=0)
    return rows[:, :feat].astype(BF), rows[:, feat : feat + 1]


def resid_kernel(*refs):
    out_ref, resid_ref = refs[-2:]
    feat, tokens = out_ref.shape[1:]
    change, pos = back_rows(refs[:-2], feat)
    change = contract_rows(change, one_hot(pos, tokens))
    resid_ref[0] = (out_ref[0].astype(F32) + change).astype(BF)


def plain_kernel(block_ref, w_ref, *refs):
    outs, acc_ref = refs[:-1], refs[-1]
    step = pl.program_id(0)
    groups, cores, feat, tokens = block_ref.shape
    ep = lax.axis_index("ep")

    @pl.when(step == 0)
    def _():
        acc_ref[...] = jnp.zeros_like(acc_ref)

    columns = []
    for shift in range(groups):
        g = lax.rem(ep + shift, groups)
        columns.append(jnp.concatenate([block_ref[g, c] for c in range(cores)], axis=0))
    acc_ref[...] += contract_rows(jnp.concatenate(columns, axis=1), w_ref[...])

    @pl.when(step == pl.num_programs(0) - 1)
    def _():
        for shift in range(groups):
            outs[shift][...] = acc_ref[shift * tokens : (shift + 1) * tokens, :].astype(BF)


def fixed_kernel(delta_ref, w_ref, *refs):
    outs, (acc_ref, buffer, sems) = refs[:-3], refs[-3:]
    experts, quarters, cores, rows, _ = delta_ref.shape
    groups = len(outs)
    capacity = rows // groups
    height = w_ref.shape[0] // quarters
    feat = height // cores
    ep = lax.axis_index("ep")
    copies = []
    for q in range(quarters):
        part = slice(q * height, (q + 1) * height)
        copies.append(pltpu.make_async_copy(w_ref.at[part, :], buffer.at[part, :], sems.at[q]))
        copies[-1].start()
    for q in range(quarters):
        copies[q].wait()
        total = None
        for c in range(cores):
            delta = jnp.concatenate([delta_ref[e, q, c] for e in range(experts)], axis=0)
            start = q * height + c * feat
            part = mm(delta[:, :feat], buffer[start : start + feat, :])
            total = part if total is None else total + part
        acc_ref[...] = total if q == 0 else acc_ref[...] + total
    for shift in range(groups):
        pieces = []
        for s in range(experts):
            e = lax.rem(ep + shift + s, experts)
            start = pl.multiple_of(e * rows + s * capacity, 8)
            pieces.append(acc_ref[pl.ds(start, capacity), :])
        outs[shift][...] = jnp.concatenate(pieces, axis=0).astype(BF)


def weight_kernel(block_ref, delta_ref, ctx_ref, out_ref):
    groups, cores, feat, tokens = block_ref.shape
    experts, _, _, rows, _ = delta_ref.shape
    capacity = rows // groups
    ep = lax.axis_index("ep")
    columns = experts * rows
    row = row_ids((columns, 1))
    group_of = lax.rem(row // rows - lax.rem(row // capacity, groups) + groups, groups)
    for c in range(cores):
        packed = jnp.concatenate([delta_ref[e, 0, c] for e in range(experts)], axis=0)
        delta = packed[:, :feat]
        pos = packed[:, feat : feat + 1].astype(F32)
        blocks = []
        for shift in range(groups):
            g = lax.rem(ep - shift + groups, groups)
            hot = one_hot(jnp.where(group_of == g, pos, -1.0), tokens)
            change = contract_rows(delta, hot)
            blocks.append((block_ref[g, c].astype(F32) + change).astype(BF))
        total = mm(jnp.concatenate(blocks, axis=1), ctx_ref[...])
        out_ref[c * feat : (c + 1) * feat, :] = total.astype(BF)


def context_kernel(groups, *refs):
    out_ref = refs[-1]
    tokens = out_ref.shape[2]
    backs, plains, fixes = refs[:groups], refs[groups : 2 * groups], refs[2 * groups : -1]
    pos = jnp.concatenate([b[:, b.shape[1] - 1 :] for b in backs], axis=0)
    total = plains[0][...].astype(F32)
    for ref in plains[1:]:
        total = total + ref[...].astype(F32)
    hot = one_hot(pos, tokens)
    for ref in fixes:
        total = total + contract_rows(hot, ref[...])
    out_ref[0] = total.T.astype(BF)


def shards(
    residual,
    out_grad,
    norm_gain,
    context,
    w_out,
    w_gate,
    w_up,
    w_down,
    slot_token,
    slot_count,
    slot_gate,
):
    tp_count = lax.axis_size("tp")
    ep_count = lax.axis_size("ep")
    near = tp_count // ep_count
    feat, tokens = residual.shape[1:]
    features = feat * tp_count
    experts, capacity = slot_token.shape[1:]
    groups = ep_count
    slots = experts * capacity
    rows = groups * capacity
    hidden_units = w_gate.shape[2]
    unit = hidden_units // tp_count
    atts = w_out.shape[1]
    lanes = -(-(feat + 1) // 128) * 128
    gain_row = jnp.broadcast_to(norm_gain[None, :], (8, feat))
    low = 1
    while low * low < tp_count:
        low *= 2
    high = tp_count // low
    low_groups = [[a * low + b for b in range(low)] for a in range(high)]
    high_groups = [[a * low + b for a in range(high)] for b in range(low)]

    def trade(value, members):
        return lax.all_to_all(value, "tp", 0, 0, tiled=True, axis_index_groups=members)

    ahead = [[(i, (i + s) % ep_count) for i in range(ep_count)] for s in range(ep_count)]
    behind = [[(i, (i - s) % ep_count) for i in range(ep_count)] for s in range(ep_count)]

    sends = call(
        pick_kernel,
        [shape_of((2 * capacity, lanes))] * experts,
        [slot_token, slot_count, slot_gate, residual, out_grad],
        [VMEM] * 5,
        [VMEM] * experts,
        flops=4 * slots * tokens * feat,
        limit=56,
    )
    got = [sends[0]] + [lax.ppermute(sends[s], "ep", ahead[s]) for s in range(1, ep_count)]

    route = []
    for a in range(tp_count):
        for b in range(ep_count):
            route.append((a * ep_count + b, (b * near + a % near) * ep_count + a // near))
    moved = lax.ppermute(out_grad[0], ("tp", "ep"), route)

    ctx_own = context[0].T
    ctx_parts = [ctx_own] + [lax.ppermute(ctx_own, "ep", ahead[s]) for s in range(1, ep_count)]
    ctx_all = jnp.concatenate(ctx_parts, axis=0)

    steps = 4
    tile = hidden_units // steps
    wide = 3 * unit + 128
    if unit % 128 == 0:
        (sums,) = call(
            functools.partial(parts_kernel, features, groups, steps),
            [shape_of((low, high, rows, wide))],
            got + [gain_row, w_gate, w_up, w_down],
            [VMEM] * (groups + 1) + [HBM] * 3,
            [VMEM],
            scratch=[
                pltpu.VMEM((3, feat, hidden_units), BF),
                pltpu.SemaphoreType.DMA((3, steps)),
            ],
            flops=6 * rows * feat * hidden_units,
        )
    else:
        x, go, _ = rows_of(got, feat)
        gained = (x * norm_gain[None, :]).astype(BF)
        square = jnp.sum(x * x, axis=1, keepdims=True) / features
        parts = [mm(gained, w_gate[0]), mm(gained, w_up[0]), mm(go.astype(BF), w_down[0])]
        parts = [p.astype(BF).reshape(rows, tp_count, unit).transpose(1, 0, 2) for p in parts]
        tail = two_lanes(square, (rows, 128)).astype(BF)
        tail = jnp.broadcast_to(tail[None], (tp_count, rows, 128))
        sums = jnp.concatenate(parts + [tail], axis=2)
        sums = sums.reshape(high, low, rows, wide).transpose(1, 0, 2, 3)
    moved, _ = lax.optimization_barrier((moved, got[-1]))
    block = lax.all_gather(moved, "tp", axis=0).reshape(groups, near, feat, tokens)
    sums, _ = lax.optimization_barrier((sums, moved))
    (sums,) = call(add_kernel, [shape_of((high, rows, wide))], [trade(sums, low_groups)], [VMEM], [VMEM])
    sums = trade(sums, high_groups)
    if unit % 128 == 0:
        inv_rms, acts = call(
            functools.partial(act_kernel, unit),
            [shape_of((rows, 128), F32), shape_of((high, rows, wide))],
            [sums],
            [VMEM],
            [VMEM, VMEM],
        )
    else:
        inv_rms, acts = activate(jnp.sum(sums.astype(F32), axis=0), unit)
        inv_rms = jnp.broadcast_to(inv_rms, (rows, 128))
        acts = jnp.broadcast_to(acts[None], (high,) + acts.shape)
    acts = trade(acts, high_groups)
    acts = trade(jnp.broadcast_to(acts[None], (low,) + acts.shape), low_groups)
    acts, ctx_all = lax.optimization_barrier((acts, ctx_all))
    if unit % 128 == 0:
        made = call(
            functools.partial(delta_kernel, features, unit, groups, steps),
            [shape_of((rows, hidden_units))] * 3
            + [shape_of((rows, feat))] * 2
            + [shape_of((rows, lanes))]
            + [shape_of((capacity, lanes), F32)] * groups,
            got + [acts, gain_row, inv_rms, w_gate, w_up],
            [VMEM] * (groups + 3) + [HBM] * 2,
            [VMEM] * (6 + groups),
            scratch=[
                pltpu.VMEM((2, feat, hidden_units), BF),
                pltpu.SemaphoreType.DMA((2, steps)),
            ],
            flops=4 * rows * feat * hidden_units,
        )
        hidden, d_gate, d_up, slot_in, rows_go, delta = made[:6]
        backs = list(made[6:])
    else:
        x, go, pos = rows_of(got, feat)
        rows_go = go.astype(BF)
        acts = acts.transpose(1, 0, 2, 3).reshape(tp_count, rows, wide)
        hidden, d_gate, d_up = [
            acts[:, :, n * unit : (n + 1) * unit].transpose(1, 0, 2).reshape(rows, hidden_units)
            for n in range(3)
        ]
        dots = jnp.sum(acts[:, :, 3 * unit : 3 * unit + 2].astype(F32), axis=(0, 2))[:, None]
        normed = x * inv_rms[:, :1]
        slot_in = (normed * norm_gain[None, :]).astype(BF)
        slot_back = contract_cols(d_gate, w_gate[0]) + contract_cols(d_up, w_up[0])
        change = inv_rms[:, :1] * (slot_back * norm_gain[None, :] - normed * (dots / features))
        packed = jnp.concatenate([change, jnp.broadcast_to(pos, (rows, lanes - feat))], axis=1)
        delta = packed.astype(BF)
        backs = [packed[s * capacity : (s + 1) * capacity] for s in range(groups)]

    spread = lax.ppermute(delta, ("tp", "ep"), route)
    backs = [backs[0]] + [lax.ppermute(backs[s], "ep", behind[s]) for s in range(1, ep_count)]
    grads = call(
        grads_kernel,
        [shape_of((1, feat, hidden_units))] * 3,
        [slot_in, rows_go, hidden, d_gate, d_up],
        [pl.BlockSpec((rows, feat), lambda i: (0, 0))] * 2
        + [pl.BlockSpec((rows, tile), lambda i: (0, i))] * 3,
        [pl.BlockSpec((1, feat, tile), lambda i: (0, 0, i))] * 3,
        grid=(steps,),
        flops=6 * rows * feat * hidden_units,
    )
    spread, grads = lax.optimization_barrier((spread, grads))
    spread = jnp.broadcast_to(spread[None], (tp_count, rows, lanes))
    spread = lax.all_to_all(spread, "tp", split_axis=0, concat_axis=0, tiled=True)
    spread = spread.reshape(experts, near // 2, 2, rows, lanes)

    quarters = near // 2
    out_block = pl.BlockSpec((groups, 2, feat, tokens), lambda q: (0, q, 0, 0))
    delta_block = pl.BlockSpec((experts, 1, 2, rows, lanes), lambda q: (0, q, 0, 0, 0))
    w_block = pl.BlockSpec((2 * feat, atts), lambda q: (q, 0))
    plain = call(
        plain_kernel,
        [shape_of((tokens, atts))] * groups,
        [block, w_out],
        [out_block, w_block],
        [pl.BlockSpec((tokens, atts), lambda q: (0, 0))] * groups,
        grid=(quarters,),
        scratch=[pltpu.VMEM((groups * tokens, atts), F32)],
        flops=2 * groups * tokens * near * feat * atts,
        limit=52,
    )
    spread, plain = lax.optimization_barrier((spread, plain))
    plains = [plain[0]] + [lax.ppermute(plain[s], "ep", ahead[s]) for s in range(1, ep_count)]
    fixed = call(
        fixed_kernel,
        [shape_of((slots, atts))] * groups,
        [spread, w_out],
        [VMEM, HBM],
        [VMEM] * groups,
        scratch=[
            pltpu.VMEM((experts * rows, atts), F32),
            pltpu.VMEM(w_out.shape, BF),
            pltpu.SemaphoreType.DMA((quarters,)),
        ],
        flops=2 * experts * rows * near * feat * atts,
        limit=52,
    )
    spread, fixed = lax.optimization_barrier((spread, fixed))
    fixes = [fixed[0]] + [lax.ppermute(fixed[s], "ep", ahead[s]) for s in range(1, ep_count)]
    (w_out_grad,) = call(
        weight_kernel,
        [shape_of((near * feat, atts))],
        [block, spread, ctx_all],
        [out_block, delta_block, pl.BlockSpec(ctx_all.shape, lambda q: (0, 0))],
        [pl.BlockSpec((2 * feat, atts), lambda q: (q, 0))],
        grid=(quarters,),
        flops=2 * groups * tokens * near * feat * atts,
        limit=52,
    )
    (w_out_grad, backs) = lax.optimization_barrier((w_out_grad, backs))
    (resid,) = call(
        resid_kernel,
        [shape_of((1, feat, tokens))],
        backs + [out_grad],
        [VMEM] * (groups + 1),
        [VMEM],
        flops=2 * slots * feat * tokens,
    )
    (ctx_grad,) = call(
        functools.partial(context_kernel, groups),
        [shape_of((1, atts, tokens))],
        backs + plains + fixes,
        [VMEM] * (3 * groups),
        [VMEM],
        flops=2 * slots * tokens * atts,
    )
    return (resid, ctx_grad, w_out_grad) + tuple(grads)


def solution(mesh):
    return jax.shard_map(
        shards,
        mesh=mesh,
        in_specs=(
            P("ep", "tp", None),
            P("ep", "tp", None),
            P("tp"),
            P("ep", "tp", None),
            P("ep", "tp"),
            P("ep", "tp", None),
            P("ep", "tp", None),
            P("ep", "tp", None),
            P("ep", None, None),
            P("ep", None),
            P("ep", None, None),
        ),
        out_specs=(
            P("ep", "tp", None),
            P("ep", "tp", None),
            P("ep", "tp"),
            P("ep", "tp", None),
            P("ep", "tp", None),
            P("ep", "tp", None),
        ),
        check_vma=False,
    )
```

time: 472 us -> 122 us (0.26)
  waiting for transfers between devices: 326 us -> 10.1 us
  blocking collectives: 70.8 us -> 28.5 us
  matrix products: 34.9 us -> 0 us
  Pallas kernels: 0 us -> 34.1 us
  starting transfers between devices: 12.2 us -> 29.7 us
    all_gather x3 -> x1, waiting for transfers between devices: 192 us -> 0.02 us  [shards(): lax.all_gather(moved, 'tp', axis=0).reshape(groups, near, feat, tokens)]
    psum x1 -> x0, waiting for transfers between devices: 87.7 us -> none  [shards(): pre_gate, pre_up, hid_grad = lax.psum((gate_part, up_part, hid_part), 'tp')]
    psum x2 -> x0, blocking collectives: 64.4 us -> none  [the longest x1 34.9 us: shards(): square = lax.psum(jnp.sum(stream * stream, axis=0), 'tp')]
    all_to_all x3 -> x2, waiting for transfers between devices: 45.6 us -> 8.09 us  [the longest x1 5.91 us: trade(): lax.all_to_all(value, 'tp', 0, 0, tiled=True, axis_index_groups=members)]
    dot_general x13 -> x0, matrix products: 34.9 us -> none  [the longest x4 14.8 us: contract_rows(): lax.dot_general(left, right, (((0,), (0,)), ((), ())), preferred_element_...]
    pallas_call x0 -> x11, Pallas kernels: none -> 34.1 us  [call(): pl.pallas_call(kernel, out_shape=tuple(outs), in_specs=in_specs, out_spec...]
    all_to_all x1 -> x3, blocking collectives: 6.38 us -> 28.5 us  [trade(): lax.all_to_all(value, 'tp', 0, 0, tiled=True, axis_index_groups=members)]
    ppermute x0 -> x7, starting transfers between devices: none -> 19.8 us  [the longest x1 7.82 us: shards(): lax.ppermute(ctx_own, 'ep', ahead[s])]
  transfers between devices with their start and end apart: 7 -> 10, of which waited for: 7 -> 3; matrix products, arithmetic and copies ran while one was open for 5% -> 3% of each run, Pallas kernels for 0% -> 27%
where the time goes in v1:
time: 122 us; the launch traced here: 121 us
  Pallas kernels  34.1 us (28%)
  starting transfers between devices  29.7 us (24%)
  blocking collectives  28.5 us (23%)
  between operations  14.1 us (12%)
  waiting for transfers between devices  10.1 us (8%)
  local copies, waits for them, and re-layouts  4.81 us (4%)
    pallas_call x11, Pallas kernels, call(): pl.pallas_call(kernel, out_shape=tuple(outs), in_specs=in_specs, out_spec...  34.1 us
    all_to_all x3, blocking collectives, trade(): lax.all_to_all(value, 'tp', 0, 0, tiled=True, axis_index_groups=members)  28.5 us
    ppermute x1, starting transfers between devices, shards(): lax.ppermute(ctx_own, 'ep', ahead[s])  7.82 us
    all_to_all x1, starting transfers between devices, shards(): lax.all_to_all(spread, 'tp', split_axis=0, concat_axis=0, tiled=True)  6.47 us
    all_to_all x1, waiting for transfers between devices, trade(): lax.all_to_all(value, 'tp', 0, 0, tiled=True, axis_index_groups=members)  5.91 us
    ppermute x1, starting transfers between devices, shards(): lax.ppermute(sends[s], 'ep', ahead[s])  5.82 us
    all_to_all x1, starting transfers between devices, trade(): lax.all_to_all(value, 'tp', 0, 0, tiled=True, axis_index_groups=members)  3.41 us
    unnamed x9, local copies, waits for them, and re-layouts  2.67 us
  transfers between devices with their start and end apart: 10, of which 3 were waited for; matrix products, arithmetic and copies ran while one was open for 3% of the time, Pallas kernels for 27%

profile of v1, /device:TPU:0, one launch (start us, length us, event | category | flops | bytes accessed | tf_op | source)
XLA Modules:
  0.0 121.4 jit_solution(2236003419165523770)
XLA Ops:
  7.2 0.0 all-gather.3.cloned.1.call-start
  7.2 1.6 %collective-permute-start = (bf16[448,256]{1,0:T(8,128)(2,1)}, bf16[448,256]{1,0:T(8,128)(2,1)S(1)}, u32[]{:S(2)}, u32[]{:S(2)}) collective-permute-start(bf16[448,256]{1,0:T(8,128)(2,1)} %bitcast.8), channel_id=1, source_target_pairs={{0,0},{1,16},{2,2},{3,18},{4,4},{5,20},{6,6},{7,22},{8,8},{9,24},{... | collective-permute-start | bytes 688136 | tf_op jit(solution)/shard_map/ppermute | solution.py:417
  8.8 2.0 %shard_map.154 = (bf16[16,512]{1,0:T(8,128)(2,1)}, bf16[16,512]{1,0:T(8,128)(2,1)}) custom-call(s32[1,2,8]{2,1,0:T(2,128)} %token_ref.1, s32[1,2]{1,0:T(1,128)} %count_ref.1, f32[1,2,8]{2,1,0:T(2,128)} %gate_ref.1, bf16[1,448,256]{2,1,0:T(8,128)(2,1)} %resid_ref.1, bf16[1,448,256]{2,1,0:T(8,128)(2,1)} %refs_2_.1), custom_call_target="tpu_custom_call" | custom-call | flops 7340032 | bytes 491656 | tf_op jit(solution)/shard_map/pallas_call | solution.py:56
  10.8 5.8 %collective-permute-start.1 = (bf16[16,512]{1,0:T(8,128)(2,1)}, bf16[16,512]{1,0:T(8,128)(2,1)S(1)}, u32[]{:S(2)}, u32[]{:S(2)}) collective-permute-start(bf16[16,512]{1,0:T(8,128)(2,1)} %get-tuple-element.42), channel_id=1, source_target_pairs={{0,1},{1,0},{2,3},{3,2},{4,5},{5,4},{6,7},{7,6},{8,9},{9,8},{10,11... | collective-permute-start | bytes 49160 | tf_op jit(solution)/shard_map/ppermute | solution.py:411
  16.6 1.9 %collective-permute-done.1.refs_1_ = bf16[16,512]{1,0:T(8,128)(2,1)S(1)} collective-permute-done((bf16[16,512]{1,0:T(8,128)(2,1)}, bf16[16,512]{1,0:T(8,128)(2,1)S(1)}, u32[]{:S(2)}, u32[]{:S(2)}) %collective-permute-start.1) | collective-permute-done | bytes 16416 | tf_op jit(solution)/shard_map/ppermute | solution.py:411
  18.6 0.0 collective-permute-done
  18.6 0.0 copy-start.3
  18.6 0.7 copy-done.3
  19.2 0.0 all-gather.3.cloned.1.call-update
  19.3 1.2 %copy.17 = bf16[1,1024,256]{1,2,0:T(8,128)(2,1)S(1)} copy(bf16[1,1024,256]{2,1,0:T(8,128)(2,1)} %param.14) | data formatting | bytes 1048576 | tf_op args[3]
  20.5 7.8 %collective-permute-start.2 = (bf16[256,1024]{1,0:T(8,128)(2,1)S(1)}, bf16[256,1024]{1,0:T(8,128)(2,1)S(1)}, u32[]{:S(2)}, u32[]{:S(2)}) collective-permute-start(bf16[256,1024]{1,0:T(8,128)(2,1)S(1)} %bitcast.9), channel_id=1, source_target_pairs={{0,1},{1,0},{2,3},{3,2},{4,5},{5,4},{6,7},{7,6},{8,9},{9,8},{10,11... | collective-permute-start | bytes 1572872 | tf_op jit(solution)/shard_map/ppermute | solution.py:420
  28.3 0.7 broadcast_in_dim.6.refs_2_.refs_3_
  29.0 0.0 copy-start.1
  29.0 0.7 copy-done.1
  29.7 3.3 %shard_map.155 = bf16[4,4,16,512]{3,2,1,0:T(8,128)(2,1)S(1)} custom-call(bf16[16,512]{1,0:T(8,128)(2,1)S(1)} %copy-done.1, bf16[16,512]{1,0:T(8,128)(2,1)S(1)} %collective-permute-done.1.refs_1_, f32[8,448]{1,0:T(8,128)S(1)} %broadcast_in_dim.6.refs_2_.refs_3_, bf16[1,448,2048]{2,1,0:T(8,128)(2,1)} %refs_5_.3, bf16[1,448,2048]{2,1,0:T(8,128)(2,1)} %refs_6_.1, ...), custom_call_target="tpu_custom_call" | custom-call | flops 88080384 | bytes 5814272 | tf_op jit(solution)/shard_map/pallas_call | solution.py:56
  33.0 0.0 copy-start.2
  33.0 8.9 %all_to_all.25.parts_ref = bf16[4,4,16,512]{3,2,1,0:T(8,128)(2,1)S(1)} all-to-all(bf16[4,4,16,512]{3,2,1,0:T(8,128)(2,1)S(1)} %shard_map.155), channel_id=1, replica_groups={{0,2,4,6},{8,10,12,14},{16,18,20,22},{24,26,28,30},{1,3,5,7},{9,11,13,1..., dimensions={0} | all-to-all | bytes 524288 | tf_op jit(solution)/shard_map/all_to_all | solution.py:397
  42.0 10.1 %all_to_all.26.sums_ref = bf16[4,16,512]{2,1,0:T(8,128)(2,1)S(1)} all-to-all(bf16[4,16,512]{2,1,0:T(8,128)(2,1)S(1)} %shard_map.156), channel_id=1, replica_groups={{0,8,16,24},{2,10,18,26},{4,12,20,28},{6,14,22,30},{1,9,17,25},{3,11,19..., dimensions={0} | all-to-all | bytes 131072 | tf_op jit(solution)/shard_map/all_to_all | solution.py:397
  52.1 0.3 shard_map.157
  52.3 9.5 %all_to_all.27 = bf16[4,16,512]{2,1,0:T(8,128)(2,1)S(1)} all-to-all(bf16[4,16,512]{2,1,0:T(8,128)(2,1)S(1)} %get-tuple-element.46), channel_id=1, replica_groups={{0,8,16,24},{2,10,18,26},{4,12,20,28},{6,14,22,30},{1,9,17,25},{3,11,19..., dimensions={0} | all-to-all | bytes 131072 | tf_op jit(solution)/shard_map/all_to_all | solution.py:397
  61.8 0.7 broadcast_in_dim.7
  62.6 3.4 %all-to-all-start.3 = ((bf16[4,4,16,512]{3,2,1,0:T(8,128)(2,1)}), bf16[4,4,16,512]{3,2,1,0:T(8,128)(2,1)S(1)}, u32[]{:S(2)}, u32[]{:S(2)}) async-start(bf16[4,4,16,512]{3,2,1,0:T(8,128)(2,1)} %broadcast_in_dim.7), calls=%async_computation.3 | async-start | bytes 524288 | tf_op jit(solution)/shard_map/all_to_all | solution.py:397
  66.0 0.0 collective-permute-done.2
  66.0 0.1 pad_maximum_fusion.ctx_ref
  66.1 5.9 %all-to-all-done.3.refs_2_ = bf16[4,4,16,512]{3,2,1,0:T(8,128)(2,1)S(1)} async-done(((bf16[4,4,16,512]{3,2,1,0:T(8,128)(2,1)}), bf16[4,4,16,512]{3,2,1,0:T(8,128)(2,1)S(1)}, u32[]{:S(2)}, u32[]{:S(2)}) %all-to-all-start.3) | async-done | bytes 262176 | tf_op jit(solution)/shard_map/all_to_all | solution.py:397
  72.0 0.0 copy-done.2
  72.0 2.5 %shard_map.158 = (bf16[16,2048]{1,0:T(8,128)(2,1)S(1)}, bf16[16,2048]{1,0:T(8,128)(2,1)S(1)}, bf16[16,2048]{1,0:T(8,128)(2,1)S(1)}, bf16[16,448]{1,0:T(8,128)(2,...) custom-call(bf16[16,512]{1,0:T(8,128)(2,1)S(1)} %copy-done.2, ...), custom_call_target="tpu_custom_call" | custom-call | flops 58720256 | bytes 4261888 | tf_op jit(solution)/shard_map/pallas_call | solution.py:56
  74.5 0.7 collective-permute-start.3
  75.2 3.6 %shard_map.159 = (bf16[1,448,2048]{2,1,0:T(8,128)(2,1)}, bf16[1,448,2048]{2,1,0:T(8,128)(2,1)}, bf16[1,448,2048]{2,1,0:T(8,128)(2,1)}) custom-call(bf16[16,448]{1,0:T(8,128)(2,1)S(1)} %get-tuple-element.50.slot_ref, bf16[16,448]{1,0:T(8,128)(2,1)S(1)} %get-tuple-element.51.go_ref, bf16[16,2048]{1,0:T(8,128)(2,1)S(1)} %get-tuple-element.52.hidden_ref, ...), custom_call_target="tpu_custom_call" | custom-call | flops 88080384 | bytes 5730304 | tf_op jit(solution)/shard_map/pallas_call | solution.py:56
  78.8 0.0 collective-permute-done.3
  78.8 0.7 broadcast_in_dim.8
  79.5 6.5 %all-to-all-start.4 = ((bf16[16,16,512]{2,1,0:T(8,128)(2,1)}), bf16[16,16,512]{2,1,0:T(8,128)(2,1)S(1)}, u32[]{:S(2)}, u32[]{:S(2)}) async-start(bf16[16,16,512]{2,1,0:T(8,128)(2,1)} %broadcast_in_dim.8), calls=%async_computation.4 | async-start | bytes 524288 | tf_op jit(solution)/shard_map/all_to_all | solution.py:518
  86.0 0.0 all-gather.3.cloned.1.call-done
  86.0 7.8 %shard_map.160 = (bf16[256,1024]{1,0:T(8,128)(2,1)S(1)}, bf16[256,1024]{1,0:T(8,128)(2,1)S(1)}) custom-call(bf16[2,8,448,256]{3,2,1,0:T(8,128)(2,1)} %bitcast.11, bf16[3584,1024]{1,0:T(8,128)(2,1)} %w_ref.3), custom_call_target="tpu_custom_call" | custom-call | flops 3758096384 | bytes 12058624 | tf_op jit(solution)/shard_map/pallas_call | solution.py:56
  93.9 2.2 %all-to-all-done.4 = bf16[16,16,512]{2,1,0:T(8,128)(2,1)S(1)} async-done(((bf16[16,16,512]{2,1,0:T(8,128)(2,1)}), bf16[16,16,512]{2,1,0:T(8,128)(2,1)S(1)}, u32[]{:S(2)}, u32[]{:S(2)}) %all-to-all-start.4) | async-done | bytes 262176 | tf_op jit(solution)/shard_map/all_to_all | solution.py:518
  96.1 1.8 %collective-permute-start.5 = (bf16[256,1024]{1,0:T(8,128)(2,1)S(1)}, bf16[256,1024]{1,0:T(8,128)(2,1)S(1)}, u32[]{:S(2)}, u32[]{:S(2)}) collective-permute-start(bf16[256,1024]{1,0:T(8,128)(2,1)S(1)} %get-tuple-element.71), channel_id=1, source_target_pairs={{0,1},{1,0},{2,3},{3,2},{4,5},{5,4},{6,7},{7,6},{8,9},{9,8},{10,11... | collective-permute-start | bytes 1572872 | tf_op jit(solution)/shard_map/ppermute | solution.py:537
  97.9 0.2 collective-permute-start.4
  98.1 3.6 %shard_map.161 = (bf16[16,1024]{1,0:T(8,128)(2,1)S(1)}, bf16[16,1024]{1,0:T(8,128)(2,1)S(1)}) custom-call(bf16[2,4,2,16,512]{4,3,2,1,0:T(8,128)(2,1)S(1)} %bitcast.6, bf16[3584,1024]{1,0:T(8,128)(2,1)} %w_ref.3), custom_call_target="tpu_custom_call" | custom-call | flops 234881024 | bytes 7667712 | tf_op jit(solution)/shard_map/pallas_call | solution.py:56
  101.7 0.0 copy-start
  101.7 1.9 %collective-permute-start.6 = (bf16[16,1024]{1,0:T(8,128)(2,1)S(1)}, bf16[16,1024]{1,0:T(8,128)(2,1)S(1)}, u32[]{:S(2)}, u32[]{:S(2)}) collective-permute-start(bf16[16,1024]{1,0:T(8,128)(2,1)S(1)} %get-tuple-element.73), channel_id=1, source_target_pairs={{0,1},{1,0},{2,3},{3,2},{4,5},{5,4},{6,7},{7,6},{8,9},{9,8},{10,11... | collective-permute-start | bytes 98312 | tf_op jit(solution)/shard_map/ppermute | solution.py:553
  103.6 8.6 %shard_map.162 = bf16[3584,1024]{1,0:T(8,128)(2,1)} custom-call(bf16[2,8,448,256]{3,2,1,0:T(8,128)(2,1)} %bitcast.12, bf16[2,4,2,16,512]{4,3,2,1,0:T(8,128)(2,1)S(1)} %bitcast.7, bf16[512,1024]{1,0:T(8,128)(2,1)S(1)} %pad_maximum_fusion.ctx_ref), custom_call_target="tpu_custom_call" | custom-call | flops 3758096384 | bytes 12320768 | tf_op jit(solution)/shard_map/pallas_call | solution.py:56
  112.2 0.0 collective-permute-done.4.refs_1_
  112.2 0.0 copy-done
  112.2 1.0 shard_map.163
  113.2 0.0 collective-permute-done.6.refs_5_
  113.2 0.0 collective-permute-done.5.refs_3_
  113.2 1.4 %shard_map.164 = bf16[1,1024,256]{2,1,0:T(8,128)(2,1)} custom-call(f32[8,512]{1,0:T(8,128)S(1)} %get-tuple-element.68.refs_0_, f32[8,512]{1,0:T(8,128)S(1)} %collective-permute-done.4.refs_1_, bf16[256,1024]{1,0:T(8,128)(2,1)S(1)} %get-tuple-element.70.refs_2_, bf16[256,1024]{1,0:T(8,128)(2,1)S(1)} %collective-permute-done.5.refs_3_, ...), custom_call_target="tpu_custom_call" | custom-call | flops 8388608 | bytes 1671168 | tf_op jit(solution)/shard_map/pallas_call | solution.py:56
  (1 shorter events, 0.0 us)
Async XLA Ops:
  7.2 78.9 %all-gather.3.cloned.1.call-start = ((), (), s32[]{:S(2)}) async-start(), calls=%async_computation.5 | async-start | bytes 3899392 | tf_op jit(solution)/shard_map/all_gather | solution.py:450
  7.2 11.3 %collective-permute-start = (bf16[448,256]{1,0:T(8,128)(2,1)}, bf16[448,256]{1,0:T(8,128)(2,1)S(1)}, u32[]{:S(2)}, u32[]{:S(2)}) collective-permute-start(bf16[448,256]{1,0:T(8,128)(2,1)} %bitcast.8), channel_id=1, source_target_pairs={{0,0},{1,16},{2,2},{3,18},{4,4},{5,20},{6,6},{7,22},{8,8},{9,24},{... | collective-permute-start | bytes 688136 | tf_op jit(solution)/shard_map/ppermute | solution.py:417
  10.8 7.7 %collective-permute-start.1 = (bf16[16,512]{1,0:T(8,128)(2,1)}, bf16[16,512]{1,0:T(8,128)(2,1)S(1)}, u32[]{:S(2)}, u32[]{:S(2)}) collective-permute-start(bf16[16,512]{1,0:T(8,128)(2,1)} %get-tuple-element.42), channel_id=1, source_target_pairs={{0,1},{1,0},{2,3},{3,2},{4,5},{5,4},{6,7},{7,6},{8,9},{9,8},{10,11... | collective-permute-start | bytes 49160 | tf_op jit(solution)/shard_map/ppermute | solution.py:411
  18.6 0.7 copy-start.3
  20.5 45.5 %collective-permute-start.2 = (bf16[256,1024]{1,0:T(8,128)(2,1)S(1)}, bf16[256,1024]{1,0:T(8,128)(2,1)S(1)}, u32[]{:S(2)}, u32[]{:S(2)}) collective-permute-start(bf16[256,1024]{1,0:T(8,128)(2,1)S(1)} %bitcast.9), channel_id=1, source_target_pairs={{0,1},{1,0},{2,3},{3,2},{4,5},{5,4},{6,7},{7,6},{8,9},{9,8},{10,11... | collective-permute-start | bytes 1572872 | tf_op jit(solution)/shard_map/ppermute | solution.py:420
  29.0 0.7 copy-start.1
  33.0 39.0 %copy-start.2 = (bf16[16,512]{1,0:T(8,128)(2,1)S(1)}, bf16[16,512]{1,0:T(8,128)(2,1)}, u32[]{:S(2)}) copy-start(bf16[16,512]{1,0:T(8,128)(2,1)} %get-tuple-element.44.refs_0_) | copy-start | bytes 49156
  62.6 9.4 %all-to-all-start.3 = ((bf16[4,4,16,512]{3,2,1,0:T(8,128)(2,1)}), bf16[4,4,16,512]{3,2,1,0:T(8,128)(2,1)S(1)}, u32[]{:S(2)}, u32[]{:S(2)}) async-start(bf16[4,4,16,512]{3,2,1,0:T(8,128)(2,1)} %broadcast_in_dim.7), calls=%async_computation.3 | async-start | bytes 524288 | tf_op jit(solution)/shard_map/all_to_all | solution.py:397
  74.5 4.3 %collective-permute-start.3 = (bf16[16,512]{1,0:T(8,128)(2,1)S(1)}, bf16[16,512]{1,0:T(8,128)(2,1)S(1)}, u32[]{:S(2)}, u32[]{:S(2)}) collective-permute-start(bf16[16,512]{1,0:T(8,128)(2,1)S(1)} %get-tuple-element.49), channel_id=1, source_target_pairs={{0,0},{1,16},{2,2},{3,18},{4,4},{5,20},{6,6},{7,22},{8,8},{9,24},{... | collective-permute-start | bytes 49160 | tf_op jit(solution)/shard_map/ppermute | solution.py:504
  79.5 16.5 %all-to-all-start.4 = ((bf16[16,16,512]{2,1,0:T(8,128)(2,1)}), bf16[16,16,512]{2,1,0:T(8,128)(2,1)S(1)}, u32[]{:S(2)}, u32[]{:S(2)}) async-start(bf16[16,16,512]{2,1,0:T(8,128)(2,1)} %broadcast_in_dim.8), calls=%async_computation.4 | async-start | bytes 524288 | tf_op jit(solution)/shard_map/all_to_all | solution.py:518
  96.1 17.1 %collective-permute-start.5 = (bf16[256,1024]{1,0:T(8,128)(2,1)S(1)}, bf16[256,1024]{1,0:T(8,128)(2,1)S(1)}, u32[]{:S(2)}, u32[]{:S(2)}) collective-permute-start(bf16[256,1024]{1,0:T(8,128)(2,1)S(1)} %get-tuple-element.71), channel_id=1, source_target_pairs={{0,1},{1,0},{2,3},{3,2},{4,5},{5,4},{6,7},{7,6},{8,9},{9,8},{10,11... | collective-permute-start | bytes 1572872 | tf_op jit(solution)/shard_map/ppermute | solution.py:537
  97.9 14.4 %collective-permute-start.4 = (f32[8,512]{1,0:T(8,128)S(1)}, f32[8,512]{1,0:T(8,128)S(1)}, u32[]{:S(2)}, u32[]{:S(2)}) collective-permute-start(f32[8,512]{1,0:T(8,128)S(1)} %get-tuple-element.67), channel_id=1, source_target_pairs={{0,1},{1,0},{2,3},{3,2},{4,5},{5,4},{6,7},{7,6},{8,9},{9,8},{10,11... | collective-permute-start | bytes 49160 | tf_op jit(solution)/shard_map/ppermute | solution.py:505
  101.7 10.5 %copy-start = (bf16[1,448,256]{2,1,0:T(8,128)(2,1)S(1)}, bf16[1,448,256]{2,1,0:T(8,128)(2,1)}, u32[]{:S(2)}) copy-start(bf16[1,448,256]{2,1,0:T(8,128)(2,1)} %refs_2_.1) | copy-start | bytes 688132
  101.7 11.5 %collective-permute-start.6 = (bf16[16,1024]{1,0:T(8,128)(2,1)S(1)}, bf16[16,1024]{1,0:T(8,128)(2,1)S(1)}, u32[]{:S(2)}, u32[]{:S(2)}) collective-permute-start(bf16[16,1024]{1,0:T(8,128)(2,1)S(1)} %get-tuple-element.73), channel_id=1, source_target_pairs={{0,1},{1,0},{2,3},{3,2},{4,5},{5,4},{6,7},{7,6},{8,9},{9,8},{10,11... | collective-permute-start | bytes 98312 | tf_op jit(solution)/shard_map/ppermute | solution.py:553
Sparse Core Ops, SparseCore 0:
  19.4 55.3 all-gather.2

commit v2 on v1

--- a/solution.py
+++ b/solution.py
@@ -78,7 +78,7 @@
     return jnp.where(hit, 1.0, 0.0).astype(BF)
 
 
-def pick_kernel(token_ref, count_ref, gate_ref, resid_ref, out_ref, *sends):
+def pick_kernel(token_ref, count_ref, gate_ref, resid_ref, out_ref, gain_ref, *sends):
     experts, capacity = token_ref.shape[1:]
     feat, tokens = resid_ref.shape[1:]
     lanes = sends[0].shape[1]
@@ -110,20 +110,24 @@
     hot = one_hot(pos, tokens)
     picked = contract_cols(hot, resid_ref[0])
     grads = column(gate_ref) * contract_cols(hot, out_ref[0])
+    gained = picked * gain_ref[...]
     for s in range(experts):
         rows = slice(s * capacity, (s + 1) * capacity)
-        sends[s][:, :feat] = jnp.concatenate([picked[rows], grads[rows]], axis=0).astype(BF)
-        tail = jnp.concatenate([pos[rows], pos[rows]], axis=0)
-        sends[s][:, feat:] = jnp.broadcast_to(tail, (2 * capacity, lanes - feat)).astype(BF)
+        body = [picked[rows], grads[rows], gained[rows], gained[rows]]
+        sends[s][:, :feat] = jnp.concatenate(body, axis=0).astype(BF)
+        tail = jnp.concatenate([pos[rows]] * 4, axis=0)
+        sends[s][:, feat:] = jnp.broadcast_to(tail, (4 * capacity, lanes - feat)).astype(BF)
 
 
 def rows_of(blocks, feat):
     blocks = [b[...].astype(F32) for b in blocks]
-    capacity = blocks[0].shape[0] // 2
-    x = jnp.concatenate([b[:capacity, :feat] for b in blocks], axis=0)
-    go = jnp.concatenate([b[capacity:, :feat] for b in blocks], axis=0)
+    capacity = blocks[0].shape[0] // 4
+    parts = [
+        jnp.concatenate([b[k * capacity : (k + 1) * capacity, :feat] for b in blocks], axis=0)
+        for k in range(3)
+    ]
     pos = jnp.concatenate([b[:capacity, feat : feat + 1] for b in blocks], axis=0)
-    return x, go, pos
+    return parts + [pos]
 
 
 def fetch(sources, buffer, sems, steps):
@@ -145,16 +149,15 @@
 
 def parts_kernel(features, groups, steps, *refs):
     got = refs[:groups]
-    gain_ref, gate_ref, up_ref, down_ref, sums_ref, buffer, sems = refs[groups:]
+    gate_ref, up_ref, down_ref, sums_ref, buffer, sems = refs[groups:]
     copies = fetch((gate_ref, up_ref, down_ref), buffer, sems, steps)
     feat = buffer.shape[1]
-    low, high, _, lanes = sums_ref.shape
-    count = low * high
+    count, _, lanes = sums_ref.shape
     unit = buffer.shape[2] // count
     chunk = count // steps
     tile = unit * chunk
-    x, go, _ = rows_of(got, feat)
-    gained = (x * gain_ref[:1]).astype(BF)
+    x, go, gained, _ = rows_of(got, feat)
+    gained = gained.astype(BF)
     go = go.astype(BF)
     square = jnp.sum(x * x, axis=1, keepdims=True) / features
     tail = two_lanes(square, (x.shape[0], lanes - 3 * unit)).astype(BF)
@@ -165,17 +168,10 @@
             for k in range(chunk):
                 u = i * chunk + k
                 place = slice(n * unit, (n + 1) * unit)
-                sums_ref[u % low, u // low, :, place] = part[:, k * unit : (k + 1) * unit]
+                sums_ref[u, :, place] = part[:, k * unit : (k + 1) * unit]
         for k in range(chunk):
             u = i * chunk + k
-            sums_ref[u % low, u // low, :, 3 * unit :] = tail
-
-
-def add_kernel(parts_ref, total_ref):
-    total = parts_ref[0].astype(F32)
-    for k in range(1, parts_ref.shape[0]):
-        total = total + parts_ref[k].astype(F32)
-    total_ref[...] = total.astype(BF)
+            sums_ref[u, :, 3 * unit :] = tail
 
 
 def activate(sums, unit):
@@ -214,18 +210,17 @@
     buffer, sems = refs[2 * groups + 11 :]
     copies = fetch((gate_ref, up_ref), buffer, sems, steps)
     feat = buffer.shape[1]
-    low, high = acts_ref.shape[:2]
-    count = low * high
+    count = acts_ref.shape[0]
     chunk = count // steps
     tile = unit * chunk
-    x, go, pos = rows_of(got, feat)
+    x, go, _, pos = rows_of(got, feat)
     inv_rms = inv_ref[:, :1]
     normed = x * inv_rms
     slot_ref[...] = (normed * gain_ref[:1]).astype(BF)
     go_ref[...] = go.astype(BF)
-    dots = acts_ref[0, 0, :, 3 * unit : 3 * unit + 128].astype(F32)
+    dots = acts_ref[0, :, 3 * unit : 3 * unit + 128].astype(F32)
     for u in range(1, count):
-        dots = dots + acts_ref[u % low, u // low, :, 3 * unit : 3 * unit + 128].astype(F32)
+        dots = dots + acts_ref[u, :, 3 * unit : 3 * unit + 128].astype(F32)
     dots = (dots[:, :1] + dots[:, 1:2]) / features
     total = jnp.zeros((x.shape[0], feat), F32)
     for i in range(steps):
@@ -233,7 +228,7 @@
         for n, ref in enumerate((hidden_ref, dgate_ref, dup_ref)):
             place = slice(n * unit, (n + 1) * unit)
             value = jnp.concatenate(
-                [acts_ref[u % low, u // low, :, place] for u in range(i * chunk, (i + 1) * chunk)],
+                [acts_ref[u, :, place] for u in range(i * chunk, (i + 1) * chunk)],
                 axis=1,
             )
             ref[:, part] = value
@@ -297,23 +292,19 @@
     experts, quarters, cores, rows, _ = delta_ref.shape
     groups = len(outs)
     capacity = rows // groups
-    height = w_ref.shape[0] // quarters
-    feat = height // cores
+    feat = w_ref.shape[0] // (quarters * cores)
     ep = lax.axis_index("ep")
     copies = []
-    for q in range(quarters):
-        part = slice(q * height, (q + 1) * height)
-        copies.append(pltpu.make_async_copy(w_ref.at[part, :], buffer.at[part, :], sems.at[q]))
+    for j in range(quarters * cores):
+        part = slice(j * feat, (j + 1) * feat)
+        copies.append(pltpu.make_async_copy(w_ref.at[part, :], buffer.at[part, :], sems.at[j]))
         copies[-1].start()
-    for q in range(quarters):
-        copies[q].wait()
-        total = None
-        for c in range(cores):
-            delta = jnp.concatenate([delta_ref[e, q, c] for e in range(experts)], axis=0)
-            start = q * height + c * feat
-            part = mm(delta[:, :feat], buffer[start : start + feat, :])
-            total = part if total is None else total + part
-        acc_ref[...] = total if q == 0 else acc_ref[...] + total
+    for j in range(quarters * cores):
+        delta = [delta_ref[e, j // cores, j % cores] for e in range(experts)]
+        delta = jnp.concatenate(delta, axis=0)[:, :feat]
+        copies[j].wait()
+        part = mm(delta, buffer[j * feat : (j + 1) * feat, :])
+        acc_ref[...] = part if j == 0 else acc_ref[...] + part
     for shift in range(groups):
         pieces = []
         for s in range(experts):
@@ -331,18 +322,18 @@
     columns = experts * rows
     row = row_ids((columns, 1))
     group_of = lax.rem(row // rows - lax.rem(row // capacity, groups) + groups, groups)
+    order = [lax.rem(ep - shift + groups, groups) for shift in range(groups)]
+    packed = jnp.concatenate([delta_ref[e, 0, 0] for e in range(experts)], axis=0)
+    pos = packed[:, feat : feat + 1].astype(F32)
+    hot = jnp.concatenate(
+        [one_hot(jnp.where(group_of == g, pos, -1.0), tokens) for g in order], axis=1
+    )
+    blocks = []
     for c in range(cores):
-        packed = jnp.concatenate([delta_ref[e, 0, c] for e in range(experts)], axis=0)
-        delta = packed[:, :feat]
-        pos = packed[:, feat : feat + 1].astype(F32)
-        blocks = []
-        for shift in range(groups):
-            g = lax.rem(ep - shift + groups, groups)
-            hot = one_hot(jnp.where(group_of == g, pos, -1.0), tokens)
-            change = contract_rows(delta, hot)
-            blocks.append((block_ref[g, c].astype(F32) + change).astype(BF))
-        total = mm(jnp.concatenate(blocks, axis=1), ctx_ref[...])
-        out_ref[c * feat : (c + 1) * feat, :] = total.astype(BF)
+        delta = jnp.concatenate([delta_ref[e, 0, c] for e in range(experts)], axis=0)[:, :feat]
+        plain = jnp.concatenate([block_ref[g, c] for g in order], axis=1)
+        blocks.append((plain.astype(F32) + contract_rows(delta, hot)).astype(BF))
+    out_ref[...] = mm(jnp.concatenate(blocks, axis=0), ctx_ref[...]).astype(BF)
 
 
 def context_kernel(groups, *refs):
@@ -385,25 +376,15 @@
     unit = hidden_units // tp_count
     atts = w_out.shape[1]
     lanes = -(-(feat + 1) // 128) * 128
-    gain_row = jnp.broadcast_to(norm_gain[None, :], (8, feat))
-    low = 1
-    while low * low < tp_count:
-        low *= 2
-    high = tp_count // low
-    low_groups = [[a * low + b for b in range(low)] for a in range(high)]
-    high_groups = [[a * low + b for a in range(high)] for b in range(low)]
-
-    def trade(value, members):
-        return lax.all_to_all(value, "tp", 0, 0, tiled=True, axis_index_groups=members)
-
+    gain_row = norm_gain[None, :]
     ahead = [[(i, (i + s) % ep_count) for i in range(ep_count)] for s in range(ep_count)]
     behind = [[(i, (i - s) % ep_count) for i in range(ep_count)] for s in range(ep_count)]
 
     sends = call(
         pick_kernel,
-        [shape_of((2 * capacity, lanes))] * experts,
-        [slot_token, slot_count, slot_gate, residual, out_grad],
-        [VMEM] * 5,
+        [shape_of((4 * capacity, lanes))] * experts,
+        [slot_token, slot_count, slot_gate, residual, out_grad, norm_gain[None, :]],
+        [VMEM] * 6,
         [VMEM] * experts,
         flops=4 * slots * tokens * feat,
         limit=56,
@@ -415,10 +396,6 @@
         for b in range(ep_count):
             route.append((a * ep_count + b, (b * near + a % near) * ep_count + a // near))
     moved = lax.ppermute(out_grad[0], ("tp", "ep"), route)
-
-    ctx_own = context[0].T
-    ctx_parts = [ctx_own] + [lax.ppermute(ctx_own, "ep", ahead[s]) for s in range(1, ep_count)]
-    ctx_all = jnp.concatenate(ctx_parts, axis=0)
 
     steps = 4
     tile = hidden_units // steps
@@ -426,9 +403,9 @@
     if unit % 128 == 0:
         (sums,) = call(
             functools.partial(parts_kernel, features, groups, steps),
-            [shape_of((low, high, rows, wide))],
-            got + [gain_row, w_gate, w_up, w_down],
-            [VMEM] * (groups + 1) + [HBM] * 3,
+            [shape_of((tp_count, rows, wide))],
+            got + [w_gate, w_up, w_down],
+            [VMEM] * groups + [HBM] * 3,
             [VMEM],
             scratch=[
                 pltpu.VMEM((3, feat, hidden_units), BF),
@@ -437,24 +414,21 @@
             flops=6 * rows * feat * hidden_units,
         )
     else:
-        x, go, _ = rows_of(got, feat)
-        gained = (x * norm_gain[None, :]).astype(BF)
+        x, go, gained, _ = rows_of(got, feat)
+        gained = gained.astype(BF)
         square = jnp.sum(x * x, axis=1, keepdims=True) / features
         parts = [mm(gained, w_gate[0]), mm(gained, w_up[0]), mm(go.astype(BF), w_down[0])]
         parts = [p.astype(BF).reshape(rows, tp_count, unit).transpose(1, 0, 2) for p in parts]
         tail = two_lanes(square, (rows, 128)).astype(BF)
         tail = jnp.broadcast_to(tail[None], (tp_count, rows, 128))
         sums = jnp.concatenate(parts + [tail], axis=2)
-        sums = sums.reshape(high, low, rows, wide).transpose(1, 0, 2, 3)
-    moved, _ = lax.optimization_barrier((moved, got[-1]))
+    sums, moved = lax.optimization_barrier((sums, moved))
     block = lax.all_gather(moved, "tp", axis=0).reshape(groups, near, feat, tokens)
-    sums, _ = lax.optimization_barrier((sums, moved))
-    (sums,) = call(add_kernel, [shape_of((high, rows, wide))], [trade(sums, low_groups)], [VMEM], [VMEM])
-    sums = trade(sums, high_groups)
+    sums = lax.all_to_all(sums, "tp", split_axis=0, concat_axis=0, tiled=True)
     if unit % 128 == 0:
         inv_rms, acts = call(
             functools.partial(act_kernel, unit),
-            [shape_of((rows, 128), F32), shape_of((high, rows, wide))],
+            [shape_of((rows, 128), F32), shape_of((tp_count, rows, wide))],
             [sums],
             [VMEM],
             [VMEM, VMEM],
@@ -462,9 +436,13 @@
     else:
         inv_rms, acts = activate(jnp.sum(sums.astype(F32), axis=0), unit)
         inv_rms = jnp.broadcast_to(inv_rms, (rows, 128))
-        acts = jnp.broadcast_to(acts[None], (high,) + acts.shape)
-    acts = trade(acts, high_groups)
-    acts = trade(jnp.broadcast_to(acts[None], (low,) + acts.shape), low_groups)
+        acts = jnp.broadcast_to(acts[None], (tp_count,) + acts.shape)
+    acts, ctx_own = lax.optimization_barrier((acts, context[0]))
+    acts = lax.all_to_all(acts, "tp", split_axis=0, concat_axis=0, tiled=True)
+
+    ctx_own = ctx_own.T
+    ctx_parts = [ctx_own] + [lax.ppermute(ctx_own, "ep", ahead[s]) for s in range(1, ep_count)]
+    ctx_all = jnp.concatenate(ctx_parts, axis=0)
     acts, ctx_all = lax.optimization_barrier((acts, ctx_all))
     if unit % 128 == 0:
         made = call(
@@ -485,9 +463,8 @@
         hidden, d_gate, d_up, slot_in, rows_go, delta = made[:6]
         backs = list(made[6:])
     else:
-        x, go, pos = rows_of(got, feat)
+        x, go, _, pos = rows_of(got, feat)
         rows_go = go.astype(BF)
-        acts = acts.transpose(1, 0, 2, 3).reshape(tp_count, rows, wide)
         hidden, d_gate, d_up = [
             acts[:, :, n * unit : (n + 1) * unit].transpose(1, 0, 2).reshape(rows, hidden_units)
             for n in range(3)
@@ -544,7 +521,7 @@
         scratch=[
             pltpu.VMEM((experts * rows, atts), F32),
             pltpu.VMEM(w_out.shape, BF),
-            pltpu.SemaphoreType.DMA((quarters,)),
+            pltpu.SemaphoreType.DMA((near,)),
         ],
         flops=2 * experts * rows * near * feat * atts,
         limit=52,

time: 122 us -> 113 us (0.926)
  blocking collectives: 28.5 us -> 0 us
  waiting for transfers between devices: 10.1 us -> 26.5 us
  starting transfers between devices: 29.7 us -> 33.7 us
  local copies, waits for them, and re-layouts: 4.81 us -> 2.4 us
  Pallas kernels: 34.1 us -> 35.4 us
    all_to_all x3 -> x0, blocking collectives: 28.5 us -> none  [trade(): lax.all_to_all(value, 'tp', 0, 0, tiled=True, axis_index_groups=members)]
    ppermute x1, waiting for transfers between devices: 0.01 us -> 8.57 us  [shards(): lax.ppermute(ctx_own, 'ep', ahead[s])]
    all_to_all x1 -> x2, starting transfers between devices: 3.41 us -> 11.6 us  [the longest x1 7.1 us: shards(): sums = lax.all_to_all(sums, 'tp', split_axis=0, concat_axis=0, tiled=True)]
    ppermute x1, starting transfers between devices: 7.82 us -> 0.01 us  [shards(): lax.ppermute(ctx_own, 'ep', ahead[s])]
    all_to_all x1 -> x2, waiting for transfers between devices: 5.91 us -> 13.6 us  [the longest x1 12.1 us: shards(): sums = lax.all_to_all(sums, 'tp', split_axis=0, concat_axis=0, tiled=True)]
    all_to_all x1, starting transfers between devices: 6.47 us -> 10.6 us  [shards(): lax.all_to_all(spread, 'tp', split_axis=0, concat_axis=0, tiled=True)]
    broadcast_in_dim x2 -> x0, local copies, waits for them, and re-layouts: 1.41 us -> none  [the longest x1 0.73 us: shards(): acts = trade(jnp.broadcast_to(acts[None], (low,) + acts.shape), low_groups)]
    pallas_call x11 -> x10, Pallas kernels: 34.1 us -> 35.4 us  [call(): pl.pallas_call(kernel, out_shape=tuple(outs), in_specs=in_specs, out_spec...]
  transfers between devices with their start and end apart: 10 -> 11, of which waited for: 3 -> 6; matrix products, arithmetic and copies ran while one was open for 3% -> 1% of each run, Pallas kernels for 27% -> 30%
where the time goes in v2:
time: 113 us; the launch traced here: 112 us
  Pallas kernels  35.4 us (31%)
  starting transfers between devices  33.7 us (30%)
  waiting for transfers between devices  26.5 us (23%)
  between operations  14.2 us (13%)
  local copies, waits for them, and re-layouts  2.4 us (2%)
    pallas_call x10, Pallas kernels, call(): pl.pallas_call(kernel, out_shape=tuple(outs), in_specs=in_specs, out_spec...  35.4 us
    all_to_all x1, waiting for transfers between devices, shards(): sums = lax.all_to_all(sums, 'tp', split_axis=0, concat_axis=0, tiled=True)  12.1 us
    all_to_all x1, starting transfers between devices, shards(): lax.all_to_all(spread, 'tp', split_axis=0, concat_axis=0, tiled=True)  10.6 us
    ppermute x1, waiting for transfers between devices, shards(): lax.ppermute(ctx_own, 'ep', ahead[s])  8.57 us
    all_to_all x1, starting transfers between devices, shards(): sums = lax.all_to_all(sums, 'tp', split_axis=0, concat_axis=0, tiled=True)  7.1 us
    ppermute x1, starting transfers between devices, shards(): lax.ppermute(sends[s], 'ep', ahead[s])  5.82 us
    all_to_all x1, starting transfers between devices, shards(): acts = lax.all_to_all(acts, 'tp', split_axis=0, concat_axis=0, tiled=True)  4.49 us
  transfers between devices with their start and end apart: 11, of which 6 were waited for; matrix products, arithmetic and copies ran while one was open for 1% of the time, Pallas kernels for 30%

profile of v2, /device:TPU:0, one launch (start us, length us, event | category | flops | bytes accessed | tf_op | source)
XLA Modules:
  0.0 112.3 jit_solution(7056385525642365932)
XLA Ops:
  7.2 0.0 all-gather.3.cloned.1.call-start
  7.2 1.6 %collective-permute-start.1 = (bf16[448,256]{1,0:T(8,128)(2,1)}, bf16[448,256]{1,0:T(8,128)(2,1)S(1)}, u32[]{:S(2)}, u32[]{:S(2)}) collective-permute-start(bf16[448,256]{1,0:T(8,128)(2,1)} %bitcast.8), channel_id=1, source_target_pairs={{0,0},{1,16},{2,2},{3,18},{4,4},{5,20},{6,6},{7,22},{8,8},{9,24},{... | collective-permute-start | bytes 688136 | tf_op jit(solution)/shard_map/ppermute | solution.py:398
  8.8 2.0 %shard_map.154 = (bf16[32,512]{1,0:T(8,128)(2,1)}, bf16[32,512]{1,0:T(8,128)(2,1)}) custom-call(s32[1,2,8]{2,1,0:T(2,128)} %token_ref.1, s32[1,2]{1,0:T(1,128)} %count_ref.1, f32[1,2,8]{2,1,0:T(2,128)} %gate_ref.1, bf16[1,448,256]{2,1,0:T(8,128)(2,1)} %resid_ref.1, bf16[1,448,256]{2,1,0:T(8,128)(2,1)} %refs_2_.3, f32[1,448]{1,0:T(1,128)} %bitcast.9), custom_call_target="tpu_custom_call" | custom-call | flops 7340032 | bytes 526216 | tf_op jit(solution)/shard_map/pallas_call | solution.py:56
  10.8 5.8 %collective-permute-start = (bf16[32,512]{1,0:T(8,128)(2,1)}, bf16[32,512]{1,0:T(8,128)(2,1)S(1)}, u32[]{:S(2)}, u32[]{:S(2)}) collective-permute-start(bf16[32,512]{1,0:T(8,128)(2,1)} %get-tuple-element.45), channel_id=1, source_target_pairs={{0,1},{1,0},{2,3},{3,2},{4,5},{5,4},{6,7},{7,6},{8,9},{9,8},{10,11... | collective-permute-start | bytes 98312 | tf_op jit(solution)/shard_map/ppermute | solution.py:392
  16.6 2.1 %collective-permute-done.refs_1_ = bf16[32,512]{1,0:T(8,128)(2,1)S(1)} collective-permute-done((bf16[32,512]{1,0:T(8,128)(2,1)}, bf16[32,512]{1,0:T(8,128)(2,1)S(1)}, u32[]{:S(2)}, u32[]{:S(2)}) %collective-permute-start) | collective-permute-done | bytes 32800 | tf_op jit(solution)/shard_map/ppermute | solution.py:392
  18.7 0.0 copy-start.1
  18.7 0.8 copy-done.1
  19.5 0.0 copy-start.4
  19.5 4.0 %shard_map.155 = bf16[16,16,512]{2,1,0:T(8,128)(2,1)} custom-call(bf16[32,512]{1,0:T(8,128)(2,1)S(1)} %copy-done.1, bf16[32,512]{1,0:T(8,128)(2,1)S(1)} %collective-permute-done.refs_1_, bf16[1,448,2048]{2,1,0:T(8,128)(2,1)} %refs_5_.1, bf16[1,448,2048]{2,1,0:T(8,128)(2,1)} %refs_6_.1, bf16[1,448,2048]{2,1,0:T(8,128)(2,1)} %refs_4_.1), custom_call_target="tpu_custom_call" | custom-call | flops 88080384 | bytes 5832704 | tf_op jit(solution)/shard_map/pallas_call | solution.py:56
  23.5 0.0 collective-permute-done.1
  23.6 0.0 copy-start.5
  23.6 0.7 copy-done.5
  24.2 0.0 all-gather.3.cloned.1.call-update
  24.3 7.1 %all-to-all-start = ((bf16[16,16,512]{2,1,0:T(8,128)(2,1)}), bf16[16,16,512]{2,1,0:T(8,128)(2,1)S(1)}, u32[]{:S(2)}, u32[]{:S(2)}) async-start(bf16[16,16,512]{2,1,0:T(8,128)(2,1)} %shard_map.155), calls=%async_computation | async-start | bytes 524288 | tf_op jit(solution)/shard_map/all_to_all | solution.py:427
  31.4 0.0 copy-done.4
  31.4 0.0 copy-start.2
  31.4 0.0 copy-start.3
  31.4 0.2 copy.17
  31.6 12.1 %all-to-all-done.sums_ref = bf16[16,16,512]{2,1,0:T(8,128)(2,1)S(1)} async-done(((bf16[16,16,512]{2,1,0:T(8,128)(2,1)}), bf16[16,16,512]{2,1,0:T(8,128)(2,1)S(1)}, u32[]{:S(2)}, u32[]{:S(2)}) %all-to-all-start) | async-done | bytes 262176 | tf_op jit(solution)/shard_map/all_to_all | solution.py:427
  43.8 1.0 shard_map.156
  44.8 0.0 collective-permute-start.2
  44.8 4.5 %all-to-all-start.1 = ((bf16[16,16,512]{2,1,0:T(8,128)(2,1)}), bf16[16,16,512]{2,1,0:T(8,128)(2,1)S(1)}, u32[]{:S(2)}, u32[]{:S(2)}) async-start(bf16[16,16,512]{2,1,0:T(8,128)(2,1)} %get-tuple-element.49), calls=%async_computation.1 | async-start | bytes 524288 | tf_op jit(solution)/shard_map/all_to_all | solution.py:441
  49.3 8.6 %collective-permute-done.2 = bf16[256,1024]{1,0:T(8,128)(2,1)S(1)} collective-permute-done((bf16[256,1024]{1,0:T(8,128)(2,1)S(1)}, bf16[256,1024]{1,0:T(8,128)(2,1)S(1)}, u32[]{:S(2)}, u32[]{:S(2)}) %collective-permute-start.2) | collective-permute-done | bytes 524320 | tf_op jit(solution)/shard_map/ppermute | solution.py:444
  57.8 0.1 pad_maximum_fusion.ctx_ref
  57.9 1.4 %all-to-all-done.1.refs_2_ = bf16[16,16,512]{2,1,0:T(8,128)(2,1)S(1)} async-done(((bf16[16,16,512]{2,1,0:T(8,128)(2,1)}), bf16[16,16,512]{2,1,0:T(8,128)(2,1)S(1)}, u32[]{:S(2)}, u32[]{:S(2)}) %all-to-all-start.1) | async-done | bytes 262176 | tf_op jit(solution)/shard_map/all_to_all | solution.py:441
  59.3 0.0 copy-done.2
  59.3 0.0 copy-done.3
  59.3 2.5 %shard_map.157 = (bf16[16,2048]{1,0:T(8,128)(2,1)S(1)}, bf16[16,2048]{1,0:T(8,128)(2,1)S(1)}, bf16[16,2048]{1,0:T(8,128)(2,1)S(1)}, bf16[16,448]{1,0:T(8,128)(2,...) custom-call(bf16[32,512]{1,0:T(8,128)(2,1)S(1)} %copy-done.2, ...), custom_call_target="tpu_custom_call" | custom-call | flops 58720256 | bytes 4282112 | tf_op jit(solution)/shard_map/pallas_call | solution.py:56
  61.9 0.7 collective-permute-start.3
  62.5 3.6 %shard_map.158 = (bf16[1,448,2048]{2,1,0:T(8,128)(2,1)}, bf16[1,448,2048]{2,1,0:T(8,128)(2,1)}, bf16[1,448,2048]{2,1,0:T(8,128)(2,1)}) custom-call(bf16[16,448]{1,0:T(8,128)(2,1)S(1)} %get-tuple-element.54.slot_ref, bf16[16,448]{1,0:T(8,128)(2,1)S(1)} %get-tuple-element.55.go_ref, bf16[16,2048]{1,0:T(8,128)(2,1)S(1)} %get-tuple-element.56.hidden_ref, ...), custom_call_target="tpu_custom_call" | custom-call | flops 88080384 | bytes 5730304 | tf_op jit(solution)/shard_map/pallas_call | solution.py:56
  66.2 0.0 collective-permute-done.3
  66.2 0.7 broadcast_in_dim.5
  66.9 10.6 %all-to-all-start.2 = ((bf16[16,16,512]{2,1,0:T(8,128)(2,1)}), bf16[16,16,512]{2,1,0:T(8,128)(2,1)S(1)}, u32[]{:S(2)}, u32[]{:S(2)}) async-start(bf16[16,16,512]{2,1,0:T(8,128)(2,1)} %broadcast_in_dim.5), calls=%async_computation.2 | async-start | bytes 524288 | tf_op jit(solution)/shard_map/all_to_all | solution.py:495
  77.5 0.1 all-gather.3.cloned.1.call-done
  77.7 7.8 %shard_map.159 = (bf16[256,1024]{1,0:T(8,128)(2,1)S(1)}, bf16[256,1024]{1,0:T(8,128)(2,1)S(1)}) custom-call(bf16[2,8,448,256]{3,2,1,0:T(8,128)(2,1)} %bitcast.13, bf16[3584,1024]{1,0:T(8,128)(2,1)} %w_ref.3), custom_call_target="tpu_custom_call" | custom-call | flops 3758096384 | bytes 12058624 | tf_op jit(solution)/shard_map/pallas_call | solution.py:56
  85.5 2.1 %all-to-all-done.2 = bf16[16,16,512]{2,1,0:T(8,128)(2,1)S(1)} async-done(((bf16[16,16,512]{2,1,0:T(8,128)(2,1)}), bf16[16,16,512]{2,1,0:T(8,128)(2,1)S(1)}, u32[]{:S(2)}, u32[]{:S(2)}) %all-to-all-start.2) | async-done | bytes 262176 | tf_op jit(solution)/shard_map/all_to_all | solution.py:495
  87.6 1.3 %collective-permute-start.5 = (bf16[256,1024]{1,0:T(8,128)(2,1)S(1)}, bf16[256,1024]{1,0:T(8,128)(2,1)S(1)}, u32[]{:S(2)}, u32[]{:S(2)}) collective-permute-start(bf16[256,1024]{1,0:T(8,128)(2,1)S(1)} %get-tuple-element.75), channel_id=1, source_target_pairs={{0,1},{1,0},{2,3},{3,2},{4,5},{5,4},{6,7},{7,6},{8,9},{9,8},{10,11... | collective-permute-start | bytes 1572872 | tf_op jit(solution)/shard_map/ppermute | solution.py:514
  88.9 0.7 collective-permute-start.4
  89.6 3.4 %shard_map.160 = (bf16[16,1024]{1,0:T(8,128)(2,1)S(1)}, bf16[16,1024]{1,0:T(8,128)(2,1)S(1)}) custom-call(bf16[2,4,2,16,512]{4,3,2,1,0:T(8,128)(2,1)S(1)} %bitcast.6, bf16[3584,1024]{1,0:T(8,128)(2,1)} %w_ref.3), custom_call_target="tpu_custom_call" | custom-call | flops 234881024 | bytes 7667712 | tf_op jit(solution)/shard_map/pallas_call | solution.py:56
  93.1 0.0 copy-start
  93.1 1.4 %collective-permute-start.6 = (bf16[16,1024]{1,0:T(8,128)(2,1)S(1)}, bf16[16,1024]{1,0:T(8,128)(2,1)S(1)}, u32[]{:S(2)}, u32[]{:S(2)}) collective-permute-start(bf16[16,1024]{1,0:T(8,128)(2,1)S(1)} %get-tuple-element.77), channel_id=1, source_target_pairs={{0,1},{1,0},{2,3},{3,2},{4,5},{5,4},{6,7},{7,6},{8,9},{9,8},{10,11... | collective-permute-start | bytes 98312 | tf_op jit(solution)/shard_map/ppermute | solution.py:530
  94.4 8.6 %shard_map.161 = bf16[3584,1024]{1,0:T(8,128)(2,1)} custom-call(bf16[2,8,448,256]{3,2,1,0:T(8,128)(2,1)} %bitcast.14, bf16[2,4,2,16,512]{4,3,2,1,0:T(8,128)(2,1)S(1)} %bitcast.7, bf16[512,1024]{1,0:T(8,128)(2,1)S(1)} %pad_maximum_fusion.ctx_ref), custom_call_target="tpu_custom_call" | custom-call | flops 3758096384 | bytes 12320768 | tf_op jit(solution)/shard_map/pallas_call | solution.py:56
  103.1 0.0 collective-permute-done.4.refs_1_
  103.1 0.0 copy-done
  103.1 1.0 shard_map.162
  104.0 0.0 collective-permute-done.6.refs_5_
  104.0 0.0 collective-permute-done.5.refs_3_
  104.0 1.4 %shard_map.163 = bf16[1,1024,256]{2,1,0:T(8,128)(2,1)} custom-call(f32[8,512]{1,0:T(8,128)S(1)} %get-tuple-element.72.refs_0_, f32[8,512]{1,0:T(8,128)S(1)} %collective-permute-done.4.refs_1_, bf16[256,1024]{1,0:T(8,128)(2,1)S(1)} %get-tuple-element.74.refs_2_, bf16[256,1024]{1,0:T(8,128)(2,1)S(1)} %collective-permute-done.5.refs_3_, ...), custom_call_target="tpu_custom_call" | custom-call | flops 8388608 | bytes 1671168 | tf_op jit(solution)/shard_map/pallas_call | solution.py:56
Async XLA Ops:
  7.2 70.5 %all-gather.3.cloned.1.call-start = ((), (), s32[]{:S(2)}) async-start(), calls=%async_computation.3 | async-start | bytes 3899392 | tf_op jit(solution)/shard_map/all_gather | solution.py:426
  7.2 16.3 %collective-permute-start.1 = (bf16[448,256]{1,0:T(8,128)(2,1)}, bf16[448,256]{1,0:T(8,128)(2,1)S(1)}, u32[]{:S(2)}, u32[]{:S(2)}) collective-permute-start(bf16[448,256]{1,0:T(8,128)(2,1)} %bitcast.8), channel_id=1, source_target_pairs={{0,0},{1,16},{2,2},{3,18},{4,4},{5,20},{6,6},{7,22},{8,8},{9,24},{... | collective-permute-start | bytes 688136 | tf_op jit(solution)/shard_map/ppermute | solution.py:398
  10.8 7.9 %collective-permute-start = (bf16[32,512]{1,0:T(8,128)(2,1)}, bf16[32,512]{1,0:T(8,128)(2,1)S(1)}, u32[]{:S(2)}, u32[]{:S(2)}) collective-permute-start(bf16[32,512]{1,0:T(8,128)(2,1)} %get-tuple-element.45), channel_id=1, source_target_pairs={{0,1},{1,0},{2,3},{3,2},{4,5},{5,4},{6,7},{7,6},{8,9},{9,8},{10,11... | collective-permute-start | bytes 98312 | tf_op jit(solution)/shard_map/ppermute | solution.py:392
  18.7 0.8 copy-start.1
  19.5 11.9 %copy-start.4 = (bf16[1,1024,256]{2,1,0:T(8,128)(2,1)S(1)}, bf16[1,1024,256]{2,1,0:T(8,128)(2,1)}, u32[]{:S(2)}) copy-start(bf16[1,1024,256]{2,1,0:T(8,128)(2,1)} %param.14) | copy-start | bytes 1572868
  23.6 0.7 copy-start.5
  24.3 19.5 %all-to-all-start = ((bf16[16,16,512]{2,1,0:T(8,128)(2,1)}), bf16[16,16,512]{2,1,0:T(8,128)(2,1)S(1)}, u32[]{:S(2)}, u32[]{:S(2)}) async-start(bf16[16,16,512]{2,1,0:T(8,128)(2,1)} %shard_map.155), calls=%async_computation | async-start | bytes 524288 | tf_op jit(solution)/shard_map/all_to_all | solution.py:427
  31.4 27.9 %copy-start.2 = (bf16[32,512]{1,0:T(8,128)(2,1)S(1)}, bf16[32,512]{1,0:T(8,128)(2,1)}, u32[]{:S(2)}) copy-start(bf16[32,512]{1,0:T(8,128)(2,1)} %get-tuple-element.44.refs_0_) | copy-start | bytes 98308
  31.4 27.9 %copy-start.3 = (f32[448]{0:T(512)S(1)}, f32[448]{0:T(512)}, u32[]{:S(2)}) copy-start(f32[448]{0:T(512)} %param.13) | copy-start | bytes 5380
  44.8 13.1 %collective-permute-start.2 = (bf16[256,1024]{1,0:T(8,128)(2,1)S(1)}, bf16[256,1024]{1,0:T(8,128)(2,1)S(1)}, u32[]{:S(2)}, u32[]{:S(2)}) collective-permute-start(bf16[256,1024]{1,0:T(8,128)(2,1)S(1)} %bitcast.11), channel_id=1, source_target_pairs={{0,1},{1,0},{2,3},{3,2},{4,5},{5,4},{6,7},{7,6},{8,9},{9,8},{10,11... | collective-permute-start | bytes 1572872 | tf_op jit(solution)/shard_map/ppermute | solution.py:444
  44.8 14.6 %all-to-all-start.1 = ((bf16[16,16,512]{2,1,0:T(8,128)(2,1)}), bf16[16,16,512]{2,1,0:T(8,128)(2,1)S(1)}, u32[]{:S(2)}, u32[]{:S(2)}) async-start(bf16[16,16,512]{2,1,0:T(8,128)(2,1)} %get-tuple-element.49), calls=%async_computation.1 | async-start | bytes 524288 | tf_op jit(solution)/shard_map/all_to_all | solution.py:441
  61.9 4.3 %collective-permute-start.3 = (bf16[16,512]{1,0:T(8,128)(2,1)S(1)}, bf16[16,512]{1,0:T(8,128)(2,1)S(1)}, u32[]{:S(2)}, u32[]{:S(2)}) collective-permute-start(bf16[16,512]{1,0:T(8,128)(2,1)S(1)} %get-tuple-element.53), channel_id=1, source_target_pairs={{0,0},{1,16},{2,2},{3,18},{4,4},{5,20},{6,6},{7,22},{8,8},{9,24},{... | collective-permute-start | bytes 49160 | tf_op jit(solution)/shard_map/ppermute | solution.py:481
  66.9 20.7 %all-to-all-start.2 = ((bf16[16,16,512]{2,1,0:T(8,128)(2,1)}), bf16[16,16,512]{2,1,0:T(8,128)(2,1)S(1)}, u32[]{:S(2)}, u32[]{:S(2)}) async-start(bf16[16,16,512]{2,1,0:T(8,128)(2,1)} %broadcast_in_dim.5), calls=%async_computation.2 | async-start | bytes 524288 | tf_op jit(solution)/shard_map/all_to_all | solution.py:495
  87.6 16.4 %collective-permute-start.5 = (bf16[256,1024]{1,0:T(8,128)(2,1)S(1)}, bf16[256,1024]{1,0:T(8,128)(2,1)S(1)}, u32[]{:S(2)}, u32[]{:S(2)}) collective-permute-start(bf16[256,1024]{1,0:T(8,128)(2,1)S(1)} %get-tuple-element.75), channel_id=1, source_target_pairs={{0,1},{1,0},{2,3},{3,2},{4,5},{5,4},{6,7},{7,6},{8,9},{9,8},{10,11... | collective-permute-start | bytes 1572872 | tf_op jit(solution)/shard_map/ppermute | solution.py:514
  88.9 14.2 %collective-permute-start.4 = (f32[8,512]{1,0:T(8,128)S(1)}, f32[8,512]{1,0:T(8,128)S(1)}, u32[]{:S(2)}, u32[]{:S(2)}) collective-permute-start(f32[8,512]{1,0:T(8,128)S(1)} %get-tuple-element.71), channel_id=1, source_target_pairs={{0,1},{1,0},{2,3},{3,2},{4,5},{5,4},{6,7},{7,6},{8,9},{9,8},{10,11... | collective-permute-start | bytes 49160 | tf_op jit(solution)/shard_map/ppermute | solution.py:482
  93.1 10.0 %copy-start = (bf16[1,448,256]{2,1,0:T(8,128)(2,1)S(1)}, bf16[1,448,256]{2,1,0:T(8,128)(2,1)}, u32[]{:S(2)}) copy-start(bf16[1,448,256]{2,1,0:T(8,128)(2,1)} %refs_2_.3) | copy-start | bytes 688132
  93.1 10.9 %collective-permute-start.6 = (bf16[16,1024]{1,0:T(8,128)(2,1)S(1)}, bf16[16,1024]{1,0:T(8,128)(2,1)S(1)}, u32[]{:S(2)}, u32[]{:S(2)}) collective-permute-start(bf16[16,1024]{1,0:T(8,128)(2,1)S(1)} %get-tuple-element.77), channel_id=1, source_target_pairs={{0,1},{1,0},{2,3},{3,2},{4,5},{5,4},{6,7},{7,6},{8,9},{9,8},{10,11... | collective-permute-start | bytes 98312 | tf_op jit(solution)/shard_map/ppermute | solution.py:530
Sparse Core Ops, SparseCore 0:
  24.4 53.2 all-gather.2

commit v3 on v2

--- a/solution.py
+++ b/solution.py
@@ -257,14 +257,6 @@
     return rows[:, :feat].astype(BF), rows[:, feat : feat + 1]
 
 
-def resid_kernel(*refs):
-    out_ref, resid_ref = refs[-2:]
-    feat, tokens = out_ref.shape[1:]
-    change, pos = back_rows(refs[:-2], feat)
-    change = contract_rows(change, one_hot(pos, tokens))
-    resid_ref[0] = (out_ref[0].astype(F32) + change).astype(BF)
-
-
 def plain_kernel(block_ref, w_ref, *refs):
     outs, acc_ref = refs[:-1], refs[-1]
     step = pl.program_id(0)
@@ -337,14 +329,15 @@
 
 
 def context_kernel(groups, *refs):
-    out_ref = refs[-1]
+    grad_ref, resid_ref, out_ref = refs[-3:]
     tokens = out_ref.shape[2]
-    backs, plains, fixes = refs[:groups], refs[groups : 2 * groups], refs[2 * groups : -1]
-    pos = jnp.concatenate([b[:, b.shape[1] - 1 :] for b in backs], axis=0)
+    backs, plains, fixes = refs[:groups], refs[groups : 2 * groups], refs[2 * groups : -3]
+    change, pos = back_rows(backs, grad_ref.shape[1])
+    hot = one_hot(pos, tokens)
+    resid_ref[0] = (grad_ref[0].astype(F32) + contract_rows(change, hot)).astype(BF)
     total = plains[0][...].astype(F32)
     for ref in plains[1:]:
         total = total + ref[...].astype(F32)
-    hot = one_hot(pos, tokens)
     for ref in fixes:
         total = total + contract_rows(hot, ref[...])
     out_ref[0] = total.T.astype(BF)
@@ -395,7 +388,10 @@
     for a in range(tp_count):
         for b in range(ep_count):
             route.append((a * ep_count + b, (b * near + a % near) * ep_count + a // near))
-    moved = lax.ppermute(out_grad[0], ("tp", "ep"), route)
+    most = feat * 3 // 4 // 16 * 16
+    early = lax.ppermute(out_grad[0, :most], ("tp", "ep"), route)
+    rest, got = lax.optimization_barrier((out_grad[0, most:], got))
+    rest = lax.ppermute(rest, ("tp", "ep"), route)
 
     steps = 4
     tile = hidden_units // steps
@@ -422,7 +418,8 @@
         tail = two_lanes(square, (rows, 128)).astype(BF)
         tail = jnp.broadcast_to(tail[None], (tp_count, rows, 128))
         sums = jnp.concatenate(parts + [tail], axis=2)
-    sums, moved = lax.optimization_barrier((sums, moved))
+    sums, early, rest = lax.optimization_barrier((sums, early, rest))
+    moved = jnp.concatenate([early, rest], axis=0)
     block = lax.all_gather(moved, "tp", axis=0).reshape(groups, near, feat, tokens)
     sums = lax.all_to_all(sums, "tp", split_axis=0, concat_axis=0, tiled=True)
     if unit % 128 == 0:
@@ -538,22 +535,13 @@
         flops=2 * groups * tokens * near * feat * atts,
         limit=52,
     )
-    (w_out_grad, backs) = lax.optimization_barrier((w_out_grad, backs))
-    (resid,) = call(
-        resid_kernel,
-        [shape_of((1, feat, tokens))],
-        backs + [out_grad],
-        [VMEM] * (groups + 1),
-        [VMEM],
-        flops=2 * slots * feat * tokens,
-    )
-    (ctx_grad,) = call(
+    resid, ctx_grad = call(
         functools.partial(context_kernel, groups),
-        [shape_of((1, atts, tokens))],
-        backs + plains + fixes,
-        [VMEM] * (3 * groups),
-        [VMEM],
-        flops=2 * slots * tokens * atts,
+        [shape_of((1, feat, tokens)), shape_of((1, atts, tokens))],
+        backs + plains + fixes + [out_grad],
+        [VMEM] * (3 * groups + 1),
+        [VMEM] * 2,
+        flops=2 * slots * tokens * (atts + feat),
     )
     return (resid, ctx_grad, w_out_grad) + tuple(grads)
 

time: 113 us -> 116 us (1.027)
  starting transfers between devices: 33.7 us -> 38.1 us
  waiting for transfers between devices: 26.5 us -> 24.4 us
    all_to_all x1, starting transfers between devices: 7.1 us -> 14.5 us  [shards(): sums = lax.all_to_all(sums, 'tp', split_axis=0, concat_axis=0, tiled=True)]
    ppermute x1, starting transfers between devices: 5.82 us -> 2.94 us  [shards(): lax.ppermute(sends[s], 'ep', ahead[s])]
    ppermute x1, waiting for transfers between devices: 2.1 us -> 0.01 us  [shards(): lax.ppermute(sends[s], 'ep', ahead[s])]
    squeeze x0 -> x2, local copies, waits for them, and re-layouts: none -> 1.76 us  [the longest x1 0.93 us: shards(): early = lax.ppermute(out_grad[0, :most], ('tp', 'ep'), route)]
    pallas_call x10 -> x9, Pallas kernels: 35.4 us -> 34.5 us  [call(): pl.pallas_call(kernel, out_shape=tuple(outs), in_specs=in_specs, out_spec...]
  transfers between devices with their start and end apart: 11 -> 12, of which waited for: 6 -> 4; matrix products, arithmetic and copies ran while one was open for 1% -> 2% of each run, Pallas kernels for 30% -> 27%
where the time goes in v3:
time: 116 us; the launch traced here: 115 us
  starting transfers between devices  38.1 us (33%)
  Pallas kernels  34.5 us (30%)
  waiting for transfers between devices  24.4 us (21%)
  between operations  14.2 us (12%)
  local copies, waits for them, and re-layouts  3.47 us (3%)
    pallas_call x9, Pallas kernels, call(): pl.pallas_call(kernel, out_shape=tuple(outs), in_specs=in_specs, out_spec...  34.5 us
    all_to_all x1, starting transfers between devices, shards(): sums = lax.all_to_all(sums, 'tp', split_axis=0, concat_axis=0, tiled=True)  14.5 us
    all_to_all x1, waiting for transfers between devices, shards(): sums = lax.all_to_all(sums, 'tp', split_axis=0, concat_axis=0, tiled=True)  12.1 us
    all_to_all x1, starting transfers between devices, shards(): lax.all_to_all(spread, 'tp', split_axis=0, concat_axis=0, tiled=True)  10.6 us
    ppermute x1, waiting for transfers between devices, shards(): lax.ppermute(ctx_own, 'ep', ahead[s])  8.57 us
    all_to_all x1, starting transfers between devices, shards(): acts = lax.all_to_all(acts, 'tp', split_axis=0, concat_axis=0, tiled=True)  4.49 us
    ppermute x1, starting transfers between devices, shards(): lax.ppermute(sends[s], 'ep', ahead[s])  2.94 us
  transfers between devices with their start and end apart: 12, of which 4 were waited for; matrix products, arithmetic and copies ran while one was open for 2% of the time, Pallas kernels for 27%

profile of v3, /device:TPU:0, one launch (start us, length us, event | category | flops | bytes accessed | tf_op | source)
XLA Modules:
  0.0 115.5 jit_solution(7387477680631438747)
XLA Ops:
  7.2 0.0 all-gather.3.cloned.1.call-start
  7.2 2.0 %shard_map.154 = (bf16[32,512]{1,0:T(8,128)(2,1)}, bf16[32,512]{1,0:T(8,128)(2,1)}) custom-call(s32[1,2,8]{2,1,0:T(2,128)} %token_ref.1, s32[1,2]{1,0:T(1,128)} %count_ref.1, f32[1,2,8]{2,1,0:T(2,128)} %gate_ref.1, bf16[1,448,256]{2,1,0:T(8,128)(2,1)} %resid_ref.1, bf16[1,448,256]{2,1,0:T(8,128)(2,1)} %refs_6_.3, f32[1,448]{1,0:T(1,128)} %bitcast.11), custom_call_target="tpu_custom_call" | custom-call | flops 7340032 | bytes 526216 | tf_op jit(solution)/shard_map/pallas_call | solution.py:56
  9.2 2.9 %collective-permute-start = (bf16[32,512]{1,0:T(8,128)(2,1)}, bf16[32,512]{1,0:T(8,128)(2,1)S(1)}, u32[]{:S(2)}, u32[]{:S(2)}) collective-permute-start(bf16[32,512]{1,0:T(8,128)(2,1)} %get-tuple-element.48), channel_id=1, source_target_pairs={{0,1},{1,0},{2,3},{3,2},{4,5},{5,4},{6,7},{7,6},{8,9},{9,8},{10,11... | collective-permute-start | bytes 98312 | tf_op jit(solution)/shard_map/ppermute | solution.py:385
  12.2 0.9 slice_bitcast_fusion
  13.1 0.7 collective-permute-start.1
  13.8 0.8 slice_bitcast_fusion.1
  14.6 0.0 collective-permute-done.refs_1_
  14.6 0.7 collective-permute-start.2
  15.3 0.0 copy-start.1
  15.3 0.7 copy-done.1
  16.0 0.0 copy-start.4
  16.0 4.0 %shard_map.155 = bf16[16,16,512]{2,1,0:T(8,128)(2,1)} custom-call(bf16[32,512]{1,0:T(8,128)(2,1)S(1)} %copy-done.1, bf16[32,512]{1,0:T(8,128)(2,1)S(1)} %collective-permute-done.refs_1_, bf16[1,448,2048]{2,1,0:T(8,128)(2,1)} %refs_5_.1, bf16[1,448,2048]{2,1,0:T(8,128)(2,1)} %refs_6_.2, bf16[1,448,2048]{2,1,0:T(8,128)(2,1)} %refs_4_.1), custom_call_target="tpu_custom_call" | custom-call | flops 88080384 | bytes 5832704 | tf_op jit(solution)/shard_map/pallas_call | solution.py:56
  20.1 0.0 collective-permute-done.2
  20.1 0.0 collective-permute-done.1
  20.1 0.7 pad_maximum_fusion.1
  20.8 0.0 all-gather.3.cloned.1.call-update
  20.8 14.5 %all-to-all-start = ((bf16[16,16,512]{2,1,0:T(8,128)(2,1)}), bf16[16,16,512]{2,1,0:T(8,128)(2,1)S(1)}, u32[]{:S(2)}, u32[]{:S(2)}) async-start(bf16[16,16,512]{2,1,0:T(8,128)(2,1)} %shard_map.155), calls=%async_computation | async-start | bytes 524288 | tf_op jit(solution)/shard_map/all_to_all | solution.py:424
  35.3 0.0 copy-done.4
  35.4 0.0 copy-start.2
  35.4 0.0 copy-start.3
  35.4 0.2 copy.17
  35.6 12.1 %all-to-all-done.sums_ref = bf16[16,16,512]{2,1,0:T(8,128)(2,1)S(1)} async-done(((bf16[16,16,512]{2,1,0:T(8,128)(2,1)}), bf16[16,16,512]{2,1,0:T(8,128)(2,1)S(1)}, u32[]{:S(2)}, u32[]{:S(2)}) %all-to-all-start) | async-done | bytes 262176 | tf_op jit(solution)/shard_map/all_to_all | solution.py:424
  47.7 1.0 shard_map.156
  48.7 0.0 collective-permute-start.3
  48.7 4.5 %all-to-all-start.1 = ((bf16[16,16,512]{2,1,0:T(8,128)(2,1)}), bf16[16,16,512]{2,1,0:T(8,128)(2,1)S(1)}, u32[]{:S(2)}, u32[]{:S(2)}) async-start(bf16[16,16,512]{2,1,0:T(8,128)(2,1)} %get-tuple-element.54), calls=%async_computation.1 | async-start | bytes 524288 | tf_op jit(solution)/shard_map/all_to_all | solution.py:438
  53.2 8.6 %collective-permute-done.3 = bf16[256,1024]{1,0:T(8,128)(2,1)S(1)} collective-permute-done((bf16[256,1024]{1,0:T(8,128)(2,1)S(1)}, bf16[256,1024]{1,0:T(8,128)(2,1)S(1)}, u32[]{:S(2)}, u32[]{:S(2)}) %collective-permute-start.3) | collective-permute-done | bytes 524320 | tf_op jit(solution)/shard_map/ppermute | solution.py:441
  61.8 0.1 pad_maximum_fusion.ctx_ref
  61.9 1.5 %all-to-all-done.1.refs_2_ = bf16[16,16,512]{2,1,0:T(8,128)(2,1)S(1)} async-done(((bf16[16,16,512]{2,1,0:T(8,128)(2,1)}), bf16[16,16,512]{2,1,0:T(8,128)(2,1)S(1)}, u32[]{:S(2)}, u32[]{:S(2)}) %all-to-all-start.1) | async-done | bytes 262176 | tf_op jit(solution)/shard_map/all_to_all | solution.py:438
  63.3 0.0 copy-done.2
  63.4 0.0 copy-done.3
  63.4 2.5 %shard_map.157 = (bf16[16,2048]{1,0:T(8,128)(2,1)S(1)}, bf16[16,2048]{1,0:T(8,128)(2,1)S(1)}, bf16[16,2048]{1,0:T(8,128)(2,1)S(1)}, bf16[16,448]{1,0:T(8,128)(2,...) custom-call(bf16[32,512]{1,0:T(8,128)(2,1)S(1)} %copy-done.2, ...), custom_call_target="tpu_custom_call" | custom-call | flops 58720256 | bytes 4282112 | tf_op jit(solution)/shard_map/pallas_call | solution.py:56
  65.9 0.7 collective-permute-start.5
  66.6 3.6 %shard_map.158 = (bf16[1,448,2048]{2,1,0:T(8,128)(2,1)}, bf16[1,448,2048]{2,1,0:T(8,128)(2,1)}, bf16[1,448,2048]{2,1,0:T(8,128)(2,1)}) custom-call(bf16[16,448]{1,0:T(8,128)(2,1)S(1)} %get-tuple-element.61.slot_ref, bf16[16,448]{1,0:T(8,128)(2,1)S(1)} %get-tuple-element.62.go_ref, bf16[16,2048]{1,0:T(8,128)(2,1)S(1)} %get-tuple-element.63.hidden_ref, ...), custom_call_target="tpu_custom_call" | custom-call | flops 88080384 | bytes 5730304 | tf_op jit(solution)/shard_map/pallas_call | solution.py:56
  70.2 0.0 collective-permute-done.5
  70.2 0.7 broadcast_in_dim.5
  70.9 10.6 %all-to-all-start.2 = ((bf16[16,16,512]{2,1,0:T(8,128)(2,1)}), bf16[16,16,512]{2,1,0:T(8,128)(2,1)S(1)}, u32[]{:S(2)}, u32[]{:S(2)}) async-start(bf16[16,16,512]{2,1,0:T(8,128)(2,1)} %broadcast_in_dim.5), calls=%async_computation.2 | async-start | bytes 524288 | tf_op jit(solution)/shard_map/all_to_all | solution.py:492
  81.6 0.0 all-gather.3.cloned.1.call-done
  81.6 7.8 %shard_map.159 = (bf16[256,1024]{1,0:T(8,128)(2,1)S(1)}, bf16[256,1024]{1,0:T(8,128)(2,1)S(1)}) custom-call(bf16[2,8,448,256]{3,2,1,0:T(8,128)(2,1)} %bitcast.15, bf16[3584,1024]{1,0:T(8,128)(2,1)} %w_ref.3), custom_call_target="tpu_custom_call" | custom-call | flops 3758096384 | bytes 12058624 | tf_op jit(solution)/shard_map/pallas_call | solution.py:56
  89.4 2.2 %all-to-all-done.2 = bf16[16,16,512]{2,1,0:T(8,128)(2,1)S(1)} async-done(((bf16[16,16,512]{2,1,0:T(8,128)(2,1)}), bf16[16,16,512]{2,1,0:T(8,128)(2,1)S(1)}, u32[]{:S(2)}, u32[]{:S(2)}) %all-to-all-start.2) | async-done | bytes 262176 | tf_op jit(solution)/shard_map/all_to_all | solution.py:492
  91.6 1.4 %collective-permute-start.6 = (bf16[256,1024]{1,0:T(8,128)(2,1)S(1)}, bf16[256,1024]{1,0:T(8,128)(2,1)S(1)}, u32[]{:S(2)}, u32[]{:S(2)}) collective-permute-start(bf16[256,1024]{1,0:T(8,128)(2,1)S(1)} %get-tuple-element.75), channel_id=1, source_target_pairs={{0,1},{1,0},{2,3},{3,2},{4,5},{5,4},{6,7},{7,6},{8,9},{9,8},{10,11... | collective-permute-start | bytes 1572872 | tf_op jit(solution)/shard_map/ppermute | solution.py:511
  93.0 0.7 collective-permute-start.4
  93.6 3.4 %shard_map.160 = (bf16[16,1024]{1,0:T(8,128)(2,1)S(1)}, bf16[16,1024]{1,0:T(8,128)(2,1)S(1)}) custom-call(bf16[2,4,2,16,512]{4,3,2,1,0:T(8,128)(2,1)S(1)} %bitcast.9, bf16[3584,1024]{1,0:T(8,128)(2,1)} %w_ref.3), custom_call_target="tpu_custom_call" | custom-call | flops 234881024 | bytes 7667712 | tf_op jit(solution)/shard_map/pallas_call | solution.py:56
  97.1 0.0 copy-start
  97.1 1.4 %collective-permute-start.7 = (bf16[16,1024]{1,0:T(8,128)(2,1)S(1)}, bf16[16,1024]{1,0:T(8,128)(2,1)S(1)}, u32[]{:S(2)}, u32[]{:S(2)}) collective-permute-start(bf16[16,1024]{1,0:T(8,128)(2,1)S(1)} %get-tuple-element.80), channel_id=1, source_target_pairs={{0,1},{1,0},{2,3},{3,2},{4,5},{5,4},{6,7},{7,6},{8,9},{9,8},{10,11... | collective-permute-start | bytes 98312 | tf_op jit(solution)/shard_map/ppermute | solution.py:527
  98.5 8.6 %shard_map.162 = bf16[3584,1024]{1,0:T(8,128)(2,1)} custom-call(bf16[2,8,448,256]{3,2,1,0:T(8,128)(2,1)} %bitcast.16, bf16[2,4,2,16,512]{4,3,2,1,0:T(8,128)(2,1)S(1)} %bitcast.10, bf16[512,1024]{1,0:T(8,128)(2,1)S(1)} %pad_maximum_fusion.ctx_ref), custom_call_target="tpu_custom_call" | custom-call | flops 3758096384 | bytes 12320768 | tf_op jit(solution)/shard_map/pallas_call | solution.py:56
  107.1 0.0 collective-permute-done.4.refs_1_
  107.1 0.0 collective-permute-done.7.refs_5_
  107.1 0.0 collective-permute-done.6.refs_3_
  107.1 0.0 copy-done
  107.2 1.5 %shard_map.161 = (bf16[1,448,256]{2,1,0:T(8,128)(2,1)}, bf16[1,1024,256]{2,1,0:T(8,128)(2,1)}) custom-call(f32[8,512]{1,0:T(8,128)S(1)} %get-tuple-element.58.refs_0_, f32[8,512]{1,0:T(8,128)S(1)} %collective-permute-done.4.refs_1_, bf16[256,1024]{1,0:T(8,128)(2,1)S(1)} %get-tuple-element.74.refs_2_, bf16[256,1024]{1,0:T(8,128)(2,1)S(1)} %collective-permute-done.6.refs_3_, ...), custom_call_target="tpu_custom_call" | custom-call | flops 12058624 | bytes 2129920 | tf_op jit(solution)/shard_map/pallas_call | solution.py:56
Async XLA Ops:
  7.2 74.4 %all-gather.3.cloned.1.call-start = ((), (), s32[]{:S(2)}) async-start(), calls=%async_computation.3 | async-start | bytes 3899392 | tf_op jit(solution)/shard_map/all_gather | solution.py:423
  9.2 5.4 %collective-permute-start = (bf16[32,512]{1,0:T(8,128)(2,1)}, bf16[32,512]{1,0:T(8,128)(2,1)S(1)}, u32[]{:S(2)}, u32[]{:S(2)}) collective-permute-start(bf16[32,512]{1,0:T(8,128)(2,1)} %get-tuple-element.48), channel_id=1, source_target_pairs={{0,1},{1,0},{2,3},{3,2},{4,5},{5,4},{6,7},{7,6},{8,9},{9,8},{10,11... | collective-permute-start | bytes 98312 | tf_op jit(solution)/shard_map/ppermute | solution.py:385
  13.1 7.0 %collective-permute-start.1 = (bf16[336,256]{1,0:T(8,128)(2,1)S(1)}, bf16[336,256]{1,0:T(8,128)(2,1)S(1)}, u32[]{:S(2)}, u32[]{:S(2)}) collective-permute-start(bf16[336,256]{1,0:T(8,128)(2,1)S(1)} %slice_bitcast_fusion), channel_id=1, source_target_pairs={{0,0},{1,16},{2,2},{3,18},{4,4},{5,20},{6,6},{7,22},{8,8},{9,24},{... | collective-permute-start | bytes 516104 | tf_op jit(solution)/shard_map/ppermute | solution.py:392
  14.6 5.5 %collective-permute-start.2 = (bf16[112,256]{1,0:T(8,128)(2,1)S(1)}, bf16[112,256]{1,0:T(8,128)(2,1)S(1)}, u32[]{:S(2)}, u32[]{:S(2)}) collective-permute-start(bf16[112,256]{1,0:T(8,128)(2,1)S(1)} %slice_bitcast_fusion.1), channel_id=1, source_target_pairs={{0,0},{1,16},{2,2},{3,18},{4,4},{5,20},{6,6},{7,22},{8,8},{9,24},{... | collective-permute-start | bytes 172040 | tf_op jit(solution)/shard_map/ppermute | solution.py:394
  15.3 0.8 copy-start.1
  16.0 19.3 %copy-start.4 = (bf16[1,1024,256]{2,1,0:T(8,128)(2,1)S(1)}, bf16[1,1024,256]{2,1,0:T(8,128)(2,1)}, u32[]{:S(2)}) copy-start(bf16[1,1024,256]{2,1,0:T(8,128)(2,1)} %param.14) | copy-start | bytes 1572868
  20.8 26.9 %all-to-all-start = ((bf16[16,16,512]{2,1,0:T(8,128)(2,1)}), bf16[16,16,512]{2,1,0:T(8,128)(2,1)S(1)}, u32[]{:S(2)}, u32[]{:S(2)}) async-start(bf16[16,16,512]{2,1,0:T(8,128)(2,1)} %shard_map.155), calls=%async_computation | async-start | bytes 524288 | tf_op jit(solution)/shard_map/all_to_all | solution.py:424
  35.4 28.0 %copy-start.2 = (bf16[32,512]{1,0:T(8,128)(2,1)S(1)}, bf16[32,512]{1,0:T(8,128)(2,1)}, u32[]{:S(2)}) copy-start(bf16[32,512]{1,0:T(8,128)(2,1)} %get-tuple-element.49.refs_0_) | copy-start | bytes 98308
  35.4 28.0 %copy-start.3 = (f32[448]{0:T(512)S(1)}, f32[448]{0:T(512)}, u32[]{:S(2)}) copy-start(f32[448]{0:T(512)} %param.13) | copy-start | bytes 5380
  48.7 13.1 %collective-permute-start.3 = (bf16[256,1024]{1,0:T(8,128)(2,1)S(1)}, bf16[256,1024]{1,0:T(8,128)(2,1)S(1)}, u32[]{:S(2)}, u32[]{:S(2)}) collective-permute-start(bf16[256,1024]{1,0:T(8,128)(2,1)S(1)} %bitcast.13), channel_id=1, source_target_pairs={{0,1},{1,0},{2,3},{3,2},{4,5},{5,4},{6,7},{7,6},{8,9},{9,8},{10,11... | collective-permute-start | bytes 1572872 | tf_op jit(solution)/shard_map/ppermute | solution.py:441
  48.7 14.6 %all-to-all-start.1 = ((bf16[16,16,512]{2,1,0:T(8,128)(2,1)}), bf16[16,16,512]{2,1,0:T(8,128)(2,1)S(1)}, u32[]{:S(2)}, u32[]{:S(2)}) async-start(bf16[16,16,512]{2,1,0:T(8,128)(2,1)} %get-tuple-element.54), calls=%async_computation.1 | async-start | bytes 524288 | tf_op jit(solution)/shard_map/all_to_all | solution.py:438
  65.9 4.3 %collective-permute-start.5 = (bf16[16,512]{1,0:T(8,128)(2,1)S(1)}, bf16[16,512]{1,0:T(8,128)(2,1)S(1)}, u32[]{:S(2)}, u32[]{:S(2)}) collective-permute-start(bf16[16,512]{1,0:T(8,128)(2,1)S(1)} %get-tuple-element.60), channel_id=1, source_target_pairs={{0,0},{1,16},{2,2},{3,18},{4,4},{5,20},{6,6},{7,22},{8,8},{9,24},{... | collective-permute-start | bytes 49160 | tf_op jit(solution)/shard_map/ppermute | solution.py:478
  70.9 20.7 %all-to-all-start.2 = ((bf16[16,16,512]{2,1,0:T(8,128)(2,1)}), bf16[16,16,512]{2,1,0:T(8,128)(2,1)S(1)}, u32[]{:S(2)}, u32[]{:S(2)}) async-start(bf16[16,16,512]{2,1,0:T(8,128)(2,1)} %broadcast_in_dim.5), calls=%async_computation.2 | async-start | bytes 524288 | tf_op jit(solution)/shard_map/all_to_all | solution.py:492
  91.6 15.5 %collective-permute-start.6 = (bf16[256,1024]{1,0:T(8,128)(2,1)S(1)}, bf16[256,1024]{1,0:T(8,128)(2,1)S(1)}, u32[]{:S(2)}, u32[]{:S(2)}) collective-permute-start(bf16[256,1024]{1,0:T(8,128)(2,1)S(1)} %get-tuple-element.75), channel_id=1, source_target_pairs={{0,1},{1,0},{2,3},{3,2},{4,5},{5,4},{6,7},{7,6},{8,9},{9,8},{10,11... | collective-permute-start | bytes 1572872 | tf_op jit(solution)/shard_map/ppermute | solution.py:511
  93.0 14.2 %collective-permute-start.4 = (f32[8,512]{1,0:T(8,128)S(1)}, f32[8,512]{1,0:T(8,128)S(1)}, u32[]{:S(2)}, u32[]{:S(2)}) collective-permute-start(f32[8,512]{1,0:T(8,128)S(1)} %get-tuple-element.59), channel_id=1, source_target_pairs={{0,1},{1,0},{2,3},{3,2},{4,5},{5,4},{6,7},{7,6},{8,9},{9,8},{10,11... | collective-permute-start | bytes 49160 | tf_op jit(solution)/shard_map/ppermute | solution.py:479
  97.1 10.1 %copy-start = (bf16[1,448,256]{2,1,0:T(8,128)(2,1)S(1)}, bf16[1,448,256]{2,1,0:T(8,128)(2,1)}, u32[]{:S(2)}) copy-start(bf16[1,448,256]{2,1,0:T(8,128)(2,1)} %refs_6_.3) | copy-start | bytes 688132
  97.1 10.0 %collective-permute-start.7 = (bf16[16,1024]{1,0:T(8,128)(2,1)S(1)}, bf16[16,1024]{1,0:T(8,128)(2,1)S(1)}, u32[]{:S(2)}, u32[]{:S(2)}) collective-permute-start(bf16[16,1024]{1,0:T(8,128)(2,1)S(1)} %get-tuple-element.80), channel_id=1, source_target_pairs={{0,1},{1,0},{2,3},{3,2},{4,5},{5,4},{6,7},{7,6},{8,9},{9,8},{10,11... | collective-permute-start | bytes 98312 | tf_op jit(solution)/shard_map/ppermute | solution.py:527
Sparse Core Ops, SparseCore 0:
  20.9 60.5 all-gather.2

commit v4 on v3

--- a/solution.py
+++ b/solution.py
@@ -388,10 +388,7 @@
     for a in range(tp_count):
         for b in range(ep_count):
             route.append((a * ep_count + b, (b * near + a % near) * ep_count + a // near))
-    most = feat * 3 // 4 // 16 * 16
-    early = lax.ppermute(out_grad[0, :most], ("tp", "ep"), route)
-    rest, got = lax.optimization_barrier((out_grad[0, most:], got))
-    rest = lax.ppermute(rest, ("tp", "ep"), route)
+    moved = lax.ppermute(out_grad[0], ("tp", "ep"), route)
 
     steps = 4
     tile = hidden_units // steps
@@ -418,8 +415,7 @@
         tail = two_lanes(square, (rows, 128)).astype(BF)
         tail = jnp.broadcast_to(tail[None], (tp_count, rows, 128))
         sums = jnp.concatenate(parts + [tail], axis=2)
-    sums, early, rest = lax.optimization_barrier((sums, early, rest))
-    moved = jnp.concatenate([early, rest], axis=0)
+    sums, moved = lax.optimization_barrier((sums, moved))
     block = lax.all_gather(moved, "tp", axis=0).reshape(groups, near, feat, tokens)
     sums = lax.all_to_all(sums, "tp", split_axis=0, concat_axis=0, tiled=True)
     if unit % 128 == 0:
@@ -482,9 +478,9 @@
         [shape_of((1, feat, hidden_units))] * 3,
         [slot_in, rows_go, hidden, d_gate, d_up],
         [pl.BlockSpec((rows, feat), lambda i: (0, 0))] * 2
-        + [pl.BlockSpec((rows, tile), lambda i: (0, i))] * 3,
-        [pl.BlockSpec((1, feat, tile), lambda i: (0, 0, i))] * 3,
-        grid=(steps,),
+        + [pl.BlockSpec((rows, tile // 2), lambda i: (0, i))] * 3,
+        [pl.BlockSpec((1, feat, tile // 2), lambda i: (0, 0, i))] * 3,
+        grid=(2 * steps,),
         flops=6 * rows * feat * hidden_units,
     )
     spread, grads = lax.optimization_barrier((spread, grads))
@@ -494,7 +490,6 @@
 
     quarters = near // 2
     out_block = pl.BlockSpec((groups, 2, feat, tokens), lambda q: (0, q, 0, 0))
-    delta_block = pl.BlockSpec((experts, 1, 2, rows, lanes), lambda q: (0, q, 0, 0, 0))
     w_block = pl.BlockSpec((2 * feat, atts), lambda q: (q, 0))
     plain = call(
         plain_kernel,
@@ -528,10 +523,14 @@
     (w_out_grad,) = call(
         weight_kernel,
         [shape_of((near * feat, atts))],
-        [block, spread, ctx_all],
-        [out_block, delta_block, pl.BlockSpec(ctx_all.shape, lambda q: (0, 0))],
-        [pl.BlockSpec((2 * feat, atts), lambda q: (q, 0))],
-        grid=(quarters,),
+        [block, spread.reshape(experts, near, 1, rows, lanes), ctx_all],
+        [
+            pl.BlockSpec((groups, 1, feat, tokens), lambda j: (0, j, 0, 0)),
+            pl.BlockSpec((experts, 1, 1, rows, lanes), lambda j: (0, j, 0, 0, 0)),
+            pl.BlockSpec(ctx_all.shape, lambda j: (0, 0)),
+        ],
+        [pl.BlockSpec((feat, atts), lambda j: (j, 0))],
+        grid=(near,),
         flops=2 * groups * tokens * near * feat * atts,
         limit=52,
     )

time: 116 us -> 115 us (level)
  starting transfers between devices: 38.1 us -> 33.7 us
  Pallas kernels: 34.5 us -> 37.7 us
  waiting for transfers between devices: 24.4 us -> 26.5 us
    all_to_all x1, starting transfers between devices: 14.5 us -> 7.1 us  [shards(): sums = lax.all_to_all(sums, 'tp', split_axis=0, concat_axis=0, tiled=True)]
    pallas_call x9, Pallas kernels: 34.5 us -> 37.7 us  [call(): pl.pallas_call(kernel, out_shape=tuple(outs), in_specs=in_specs, out_spec...]
    ppermute x1, starting transfers between devices: 2.94 us -> 5.82 us  [shards(): lax.ppermute(sends[s], 'ep', ahead[s])]
    ppermute x1, waiting for transfers between devices: 0.01 us -> 2.1 us  [shards(): lax.ppermute(sends[s], 'ep', ahead[s])]
    squeeze x2 -> x0, local copies, waits for them, and re-layouts: 1.76 us -> none  [the longest x1 0.93 us: shards(): early = lax.ppermute(out_grad[0, :most], ('tp', 'ep'), route)]
  transfers between devices with their start and end apart: 12 -> 11, of which waited for: 4 -> 5; matrix products, arithmetic and copies ran while one was open for 2% -> 1% of each run, Pallas kernels for 27% -> 32%
where the time goes in v4:
time: 115 us
  Pallas kernels  37.7 us (33%)
  starting transfers between devices  33.7 us (29%)
  waiting for transfers between devices  26.5 us (23%)
  between operations  14.2 us (12%)
  local copies, waits for them, and re-layouts  2.4 us (2%)
    pallas_call x9, Pallas kernels, call(): pl.pallas_call(kernel, out_shape=tuple(outs), in_specs=in_specs, out_spec...  37.7 us
    all_to_all x1, waiting for transfers between devices, shards(): sums = lax.all_to_all(sums, 'tp', split_axis=0, concat_axis=0, tiled=True)  12.1 us
    all_to_all x1, starting transfers between devices, shards(): lax.all_to_all(spread, 'tp', split_axis=0, concat_axis=0, tiled=True)  10.6 us
    ppermute x1, waiting for transfers between devices, shards(): lax.ppermute(ctx_own, 'ep', ahead[s])  8.57 us
    all_to_all x1, starting transfers between devices, shards(): sums = lax.all_to_all(sums, 'tp', split_axis=0, concat_axis=0, tiled=True)  7.1 us
    ppermute x1, starting transfers between devices, shards(): lax.ppermute(sends[s], 'ep', ahead[s])  5.82 us
    all_to_all x1, starting transfers between devices, shards(): acts = lax.all_to_all(acts, 'tp', split_axis=0, concat_axis=0, tiled=True)  4.49 us
  transfers between devices with their start and end apart: 11, of which 5 were waited for; matrix products, arithmetic and copies ran while one was open for 1% of the time, Pallas kernels for 32%

profile of v4, /device:TPU:0, one launch (start us, length us, event | category | flops | bytes accessed | tf_op | source)
XLA Modules:
  0.0 114.5 jit_solution(1281711860806265967)
XLA Ops:
  7.2 0.0 all-gather.3.cloned.1.call-start
  7.2 1.6 %collective-permute-start.1 = (bf16[448,256]{1,0:T(8,128)(2,1)}, bf16[448,256]{1,0:T(8,128)(2,1)S(1)}, u32[]{:S(2)}, u32[]{:S(2)}) collective-permute-start(bf16[448,256]{1,0:T(8,128)(2,1)} %bitcast.9), channel_id=1, source_target_pairs={{0,0},{1,16},{2,2},{3,18},{4,4},{5,20},{6,6},{7,22},{8,8},{9,24},{... | collective-permute-start | bytes 688136 | tf_op jit(solution)/shard_map/ppermute | solution.py:391
  8.8 2.0 %shard_map.154 = (bf16[32,512]{1,0:T(8,128)(2,1)}, bf16[32,512]{1,0:T(8,128)(2,1)}) custom-call(s32[1,2,8]{2,1,0:T(2,128)} %token_ref.1, s32[1,2]{1,0:T(1,128)} %count_ref.1, f32[1,2,8]{2,1,0:T(2,128)} %gate_ref.1, bf16[1,448,256]{2,1,0:T(8,128)(2,1)} %resid_ref.1, bf16[1,448,256]{2,1,0:T(8,128)(2,1)} %refs_6_.3, f32[1,448]{1,0:T(1,128)} %bitcast.10), custom_call_target="tpu_custom_call" | custom-call | flops 7340032 | bytes 526216 | tf_op jit(solution)/shard_map/pallas_call | solution.py:56
  10.8 5.8 %collective-permute-start = (bf16[32,512]{1,0:T(8,128)(2,1)}, bf16[32,512]{1,0:T(8,128)(2,1)S(1)}, u32[]{:S(2)}, u32[]{:S(2)}) collective-permute-start(bf16[32,512]{1,0:T(8,128)(2,1)} %get-tuple-element.44), channel_id=1, source_target_pairs={{0,1},{1,0},{2,3},{3,2},{4,5},{5,4},{6,7},{7,6},{8,9},{9,8},{10,11... | collective-permute-start | bytes 98312 | tf_op jit(solution)/shard_map/ppermute | solution.py:385
  16.6 2.1 %collective-permute-done.refs_1_ = bf16[32,512]{1,0:T(8,128)(2,1)S(1)} collective-permute-done((bf16[32,512]{1,0:T(8,128)(2,1)}, bf16[32,512]{1,0:T(8,128)(2,1)S(1)}, u32[]{:S(2)}, u32[]{:S(2)}) %collective-permute-start) | collective-permute-done | bytes 32800 | tf_op jit(solution)/shard_map/ppermute | solution.py:385
  18.7 0.0 copy-start.1
  18.7 0.8 copy-done.1
  19.5 0.0 copy-start.4
  19.5 4.0 %shard_map.155 = bf16[16,16,512]{2,1,0:T(8,128)(2,1)} custom-call(bf16[32,512]{1,0:T(8,128)(2,1)S(1)} %copy-done.1, bf16[32,512]{1,0:T(8,128)(2,1)S(1)} %collective-permute-done.refs_1_, bf16[1,448,2048]{2,1,0:T(8,128)(2,1)} %refs_5_.1, bf16[1,448,2048]{2,1,0:T(8,128)(2,1)} %refs_6_.2, bf16[1,448,2048]{2,1,0:T(8,128)(2,1)} %refs_4_.1), custom_call_target="tpu_custom_call" | custom-call | flops 88080384 | bytes 5832704 | tf_op jit(solution)/shard_map/pallas_call | solution.py:56
  23.5 0.0 collective-permute-done.1
  23.6 0.0 copy-start.5
  23.6 0.7 copy-done.5
  24.2 0.0 all-gather.3.cloned.1.call-update
  24.3 7.1 %all-to-all-start = ((bf16[16,16,512]{2,1,0:T(8,128)(2,1)}), bf16[16,16,512]{2,1,0:T(8,128)(2,1)S(1)}, u32[]{:S(2)}, u32[]{:S(2)}) async-start(bf16[16,16,512]{2,1,0:T(8,128)(2,1)} %shard_map.155), calls=%async_computation | async-start | bytes 524288 | tf_op jit(solution)/shard_map/all_to_all | solution.py:420
  31.4 0.0 copy-done.4
  31.4 0.0 copy-start.2
  31.4 0.0 copy-start.3
  31.4 0.2 copy.17
  31.6 12.1 %all-to-all-done.sums_ref = bf16[16,16,512]{2,1,0:T(8,128)(2,1)S(1)} async-done(((bf16[16,16,512]{2,1,0:T(8,128)(2,1)}), bf16[16,16,512]{2,1,0:T(8,128)(2,1)S(1)}, u32[]{:S(2)}, u32[]{:S(2)}) %all-to-all-start) | async-done | bytes 262176 | tf_op jit(solution)/shard_map/all_to_all | solution.py:420
  43.8 1.0 shard_map.156
  44.8 0.0 collective-permute-start.2
  44.8 4.5 %all-to-all-start.1 = ((bf16[16,16,512]{2,1,0:T(8,128)(2,1)}), bf16[16,16,512]{2,1,0:T(8,128)(2,1)S(1)}, u32[]{:S(2)}, u32[]{:S(2)}) async-start(bf16[16,16,512]{2,1,0:T(8,128)(2,1)} %get-tuple-element.47), calls=%async_computation.1 | async-start | bytes 524288 | tf_op jit(solution)/shard_map/all_to_all | solution.py:434
  49.3 8.6 %collective-permute-done.2 = bf16[256,1024]{1,0:T(8,128)(2,1)S(1)} collective-permute-done((bf16[256,1024]{1,0:T(8,128)(2,1)S(1)}, bf16[256,1024]{1,0:T(8,128)(2,1)S(1)}, u32[]{:S(2)}, u32[]{:S(2)}) %collective-permute-start.2) | collective-permute-done | bytes 524320 | tf_op jit(solution)/shard_map/ppermute | solution.py:437
  57.8 0.1 pad_maximum_fusion.ctx_ref
  57.9 1.4 %all-to-all-done.1.refs_2_ = bf16[16,16,512]{2,1,0:T(8,128)(2,1)S(1)} async-done(((bf16[16,16,512]{2,1,0:T(8,128)(2,1)}), bf16[16,16,512]{2,1,0:T(8,128)(2,1)S(1)}, u32[]{:S(2)}, u32[]{:S(2)}) %all-to-all-start.1) | async-done | bytes 262176 | tf_op jit(solution)/shard_map/all_to_all | solution.py:434
  59.3 0.0 copy-done.2
  59.3 0.0 copy-done.3
  59.3 2.5 %shard_map.157 = (bf16[16,2048]{1,0:T(8,128)(2,1)S(1)}, bf16[16,2048]{1,0:T(8,128)(2,1)S(1)}, bf16[16,2048]{1,0:T(8,128)(2,1)S(1)}, bf16[16,448]{1,0:T(8,128)(2,...) custom-call(bf16[32,512]{1,0:T(8,128)(2,1)S(1)} %copy-done.2, ...), custom_call_target="tpu_custom_call" | custom-call | flops 58720256 | bytes 4282112 | tf_op jit(solution)/shard_map/pallas_call | solution.py:56
  61.9 0.7 collective-permute-start.4
  62.5 5.1 %shard_map.158 = (bf16[1,448,2048]{2,1,0:T(8,128)(2,1)}, bf16[1,448,2048]{2,1,0:T(8,128)(2,1)}, bf16[1,448,2048]{2,1,0:T(8,128)(2,1)}) custom-call(bf16[16,448]{1,0:T(8,128)(2,1)S(1)} %get-tuple-element.54.slot_ref, bf16[16,448]{1,0:T(8,128)(2,1)S(1)} %get-tuple-element.55.go_ref, bf16[16,2048]{1,0:T(8,128)(2,1)S(1)} %get-tuple-element.56.hidden_ref, ...), custom_call_target="tpu_custom_call" | custom-call | flops 88080384 | bytes 5730304 | tf_op jit(solution)/shard_map/pallas_call | solution.py:56
  67.6 0.0 collective-permute-done.4
  67.6 0.7 broadcast_in_dim.5
  68.3 10.6 %all-to-all-start.2 = ((bf16[16,16,512]{2,1,0:T(8,128)(2,1)}), bf16[16,16,512]{2,1,0:T(8,128)(2,1)S(1)}, u32[]{:S(2)}, u32[]{:S(2)}) async-start(bf16[16,16,512]{2,1,0:T(8,128)(2,1)} %broadcast_in_dim.5), calls=%async_computation.2 | async-start | bytes 524288 | tf_op jit(solution)/shard_map/all_to_all | solution.py:488
  79.0 0.0 all-gather.3.cloned.1.call-done
  79.0 7.8 %shard_map.159 = (bf16[256,1024]{1,0:T(8,128)(2,1)S(1)}, bf16[256,1024]{1,0:T(8,128)(2,1)S(1)}) custom-call(bf16[2,8,448,256]{3,2,1,0:T(8,128)(2,1)} %bitcast.14, bf16[3584,1024]{1,0:T(8,128)(2,1)} %w_ref.3), custom_call_target="tpu_custom_call" | custom-call | flops 3758096384 | bytes 12058624 | tf_op jit(solution)/shard_map/pallas_call | solution.py:56
  86.9 2.2 %all-to-all-done.2 = bf16[16,16,512]{2,1,0:T(8,128)(2,1)S(1)} async-done(((bf16[16,16,512]{2,1,0:T(8,128)(2,1)}), bf16[16,16,512]{2,1,0:T(8,128)(2,1)S(1)}, u32[]{:S(2)}, u32[]{:S(2)}) %all-to-all-start.2) | async-done | bytes 262176 | tf_op jit(solution)/shard_map/all_to_all | solution.py:488
  89.0 1.3 %collective-permute-start.5 = (bf16[256,1024]{1,0:T(8,128)(2,1)S(1)}, bf16[256,1024]{1,0:T(8,128)(2,1)S(1)}, u32[]{:S(2)}, u32[]{:S(2)}) collective-permute-start(bf16[256,1024]{1,0:T(8,128)(2,1)S(1)} %get-tuple-element.67), channel_id=1, source_target_pairs={{0,1},{1,0},{2,3},{3,2},{4,5},{5,4},{6,7},{7,6},{8,9},{9,8},{10,11... | collective-permute-start | bytes 1572872 | tf_op jit(solution)/shard_map/ppermute | solution.py:506
  90.3 0.7 collective-permute-start.3
  91.1 3.4 %shard_map.160 = (bf16[16,1024]{1,0:T(8,128)(2,1)S(1)}, bf16[16,1024]{1,0:T(8,128)(2,1)S(1)}) custom-call(bf16[2,4,2,16,512]{4,3,2,1,0:T(8,128)(2,1)S(1)} %bitcast.7, bf16[3584,1024]{1,0:T(8,128)(2,1)} %w_ref.3), custom_call_target="tpu_custom_call" | custom-call | flops 234881024 | bytes 7667712 | tf_op jit(solution)/shard_map/pallas_call | solution.py:56
  94.5 1.4 %collective-permute-start.6 = (bf16[16,1024]{1,0:T(8,128)(2,1)S(1)}, bf16[16,1024]{1,0:T(8,128)(2,1)S(1)}, u32[]{:S(2)}, u32[]{:S(2)}) collective-permute-start(bf16[16,1024]{1,0:T(8,128)(2,1)S(1)} %get-tuple-element.72), channel_id=1, source_target_pairs={{0,1},{1,0},{2,3},{3,2},{4,5},{5,4},{6,7},{7,6},{8,9},{9,8},{10,11... | collective-permute-start | bytes 98312 | tf_op jit(solution)/shard_map/ppermute | solution.py:522
  95.9 0.0 copy-start
  95.9 10.3 %shard_map.162 = bf16[3584,1024]{1,0:T(8,128)(2,1)} custom-call(bf16[2,8,448,256]{3,2,1,0:T(8,128)(2,1)} %bitcast.15, bf16[2,8,1,16,512]{4,3,2,1,0:T(8,128)(2,1)S(1)} %bitcast.8, bf16[512,1024]{1,0:T(8,128)(2,1)S(1)} %pad_maximum_fusion.ctx_ref), custom_call_target="tpu_custom_call" | custom-call | flops 3758096384 | bytes 12320768 | tf_op jit(solution)/shard_map/pallas_call | solution.py:56
  106.2 0.0 collective-permute-done.3.refs_1_
  106.2 0.0 collective-permute-done.6.refs_5_
  106.2 0.0 collective-permute-done.5.refs_3_
  106.2 0.0 copy-done
  106.2 1.5 %shard_map.161 = (bf16[1,448,256]{2,1,0:T(8,128)(2,1)}, bf16[1,1024,256]{2,1,0:T(8,128)(2,1)}) custom-call(f32[8,512]{1,0:T(8,128)S(1)} %get-tuple-element.51.refs_0_, f32[8,512]{1,0:T(8,128)S(1)} %collective-permute-done.3.refs_1_, bf16[256,1024]{1,0:T(8,128)(2,1)S(1)} %get-tuple-element.66.refs_2_, bf16[256,1024]{1,0:T(8,128)(2,1)S(1)} %collective-permute-done.5.refs_3_, ...), custom_call_target="tpu_custom_call" | custom-call | flops 12058624 | bytes 2129920 | tf_op jit(solution)/shard_map/pallas_call | solution.py:56
Async XLA Ops:
  7.2 71.8 %all-gather.3.cloned.1.call-start = ((), (), s32[]{:S(2)}) async-start(), calls=%async_computation.3 | async-start | bytes 3899392 | tf_op jit(solution)/shard_map/all_gather | solution.py:419
  7.2 16.3 %collective-permute-start.1 = (bf16[448,256]{1,0:T(8,128)(2,1)}, bf16[448,256]{1,0:T(8,128)(2,1)S(1)}, u32[]{:S(2)}, u32[]{:S(2)}) collective-permute-start(bf16[448,256]{1,0:T(8,128)(2,1)} %bitcast.9), channel_id=1, source_target_pairs={{0,0},{1,16},{2,2},{3,18},{4,4},{5,20},{6,6},{7,22},{8,8},{9,24},{... | collective-permute-start | bytes 688136 | tf_op jit(solution)/shard_map/ppermute | solution.py:391
  10.8 7.9 %collective-permute-start = (bf16[32,512]{1,0:T(8,128)(2,1)}, bf16[32,512]{1,0:T(8,128)(2,1)S(1)}, u32[]{:S(2)}, u32[]{:S(2)}) collective-permute-start(bf16[32,512]{1,0:T(8,128)(2,1)} %get-tuple-element.44), channel_id=1, source_target_pairs={{0,1},{1,0},{2,3},{3,2},{4,5},{5,4},{6,7},{7,6},{8,9},{9,8},{10,11... | collective-permute-start | bytes 98312 | tf_op jit(solution)/shard_map/ppermute | solution.py:385
  18.7 0.8 copy-start.1
  19.5 11.9 %copy-start.4 = (bf16[1,1024,256]{2,1,0:T(8,128)(2,1)S(1)}, bf16[1,1024,256]{2,1,0:T(8,128)(2,1)}, u32[]{:S(2)}) copy-start(bf16[1,1024,256]{2,1,0:T(8,128)(2,1)} %param.14) | copy-start | bytes 1572868
  23.6 0.7 copy-start.5
  24.3 19.5 %all-to-all-start = ((bf16[16,16,512]{2,1,0:T(8,128)(2,1)}), bf16[16,16,512]{2,1,0:T(8,128)(2,1)S(1)}, u32[]{:S(2)}, u32[]{:S(2)}) async-start(bf16[16,16,512]{2,1,0:T(8,128)(2,1)} %shard_map.155), calls=%async_computation | async-start | bytes 524288 | tf_op jit(solution)/shard_map/all_to_all | solution.py:420
  31.4 27.9 %copy-start.2 = (bf16[32,512]{1,0:T(8,128)(2,1)S(1)}, bf16[32,512]{1,0:T(8,128)(2,1)}, u32[]{:S(2)}) copy-start(bf16[32,512]{1,0:T(8,128)(2,1)} %get-tuple-element.43.refs_0_) | copy-start | bytes 98308
  31.4 27.9 %copy-start.3 = (f32[448]{0:T(512)S(1)}, f32[448]{0:T(512)}, u32[]{:S(2)}) copy-start(f32[448]{0:T(512)} %param.13) | copy-start | bytes 5380
  44.8 13.1 %collective-permute-start.2 = (bf16[256,1024]{1,0:T(8,128)(2,1)S(1)}, bf16[256,1024]{1,0:T(8,128)(2,1)S(1)}, u32[]{:S(2)}, u32[]{:S(2)}) collective-permute-start(bf16[256,1024]{1,0:T(8,128)(2,1)S(1)} %bitcast.12), channel_id=1, source_target_pairs={{0,1},{1,0},{2,3},{3,2},{4,5},{5,4},{6,7},{7,6},{8,9},{9,8},{10,11... | collective-permute-start | bytes 1572872 | tf_op jit(solution)/shard_map/ppermute | solution.py:437
  44.8 14.6 %all-to-all-start.1 = ((bf16[16,16,512]{2,1,0:T(8,128)(2,1)}), bf16[16,16,512]{2,1,0:T(8,128)(2,1)S(1)}, u32[]{:S(2)}, u32[]{:S(2)}) async-start(bf16[16,16,512]{2,1,0:T(8,128)(2,1)} %get-tuple-element.47), calls=%async_computation.1 | async-start | bytes 524288 | tf_op jit(solution)/shard_map/all_to_all | solution.py:434
  61.9 5.7 %collective-permute-start.4 = (bf16[16,512]{1,0:T(8,128)(2,1)S(1)}, bf16[16,512]{1,0:T(8,128)(2,1)S(1)}, u32[]{:S(2)}, u32[]{:S(2)}) collective-permute-start(bf16[16,512]{1,0:T(8,128)(2,1)S(1)} %get-tuple-element.53), channel_id=1, source_target_pairs={{0,0},{1,16},{2,2},{3,18},{4,4},{5,20},{6,6},{7,22},{8,8},{9,24},{... | collective-permute-start | bytes 49160 | tf_op jit(solution)/shard_map/ppermute | solution.py:474
  68.3 20.7 %all-to-all-start.2 = ((bf16[16,16,512]{2,1,0:T(8,128)(2,1)}), bf16[16,16,512]{2,1,0:T(8,128)(2,1)S(1)}, u32[]{:S(2)}, u32[]{:S(2)}) async-start(bf16[16,16,512]{2,1,0:T(8,128)(2,1)} %broadcast_in_dim.5), calls=%async_computation.2 | async-start | bytes 524288 | tf_op jit(solution)/shard_map/all_to_all | solution.py:488
  89.0 17.2 %collective-permute-start.5 = (bf16[256,1024]{1,0:T(8,128)(2,1)S(1)}, bf16[256,1024]{1,0:T(8,128)(2,1)S(1)}, u32[]{:S(2)}, u32[]{:S(2)}) collective-permute-start(bf16[256,1024]{1,0:T(8,128)(2,1)S(1)} %get-tuple-element.67), channel_id=1, source_target_pairs={{0,1},{1,0},{2,3},{3,2},{4,5},{5,4},{6,7},{7,6},{8,9},{9,8},{10,11... | collective-permute-start | bytes 1572872 | tf_op jit(solution)/shard_map/ppermute | solution.py:506
  90.3 15.9 %collective-permute-start.3 = (f32[8,512]{1,0:T(8,128)S(1)}, f32[8,512]{1,0:T(8,128)S(1)}, u32[]{:S(2)}, u32[]{:S(2)}) collective-permute-start(f32[8,512]{1,0:T(8,128)S(1)} %get-tuple-element.52), channel_id=1, source_target_pairs={{0,1},{1,0},{2,3},{3,2},{4,5},{5,4},{6,7},{7,6},{8,9},{9,8},{10,11... | collective-permute-start | bytes 49160 | tf_op jit(solution)/shard_map/ppermute | solution.py:475
  94.5 11.7 %collective-permute-start.6 = (bf16[16,1024]{1,0:T(8,128)(2,1)S(1)}, bf16[16,1024]{1,0:T(8,128)(2,1)S(1)}, u32[]{:S(2)}, u32[]{:S(2)}) collective-permute-start(bf16[16,1024]{1,0:T(8,128)(2,1)S(1)} %get-tuple-element.72), channel_id=1, source_target_pairs={{0,1},{1,0},{2,3},{3,2},{4,5},{5,4},{6,7},{7,6},{8,9},{9,8},{10,11... | collective-permute-start | bytes 98312 | tf_op jit(solution)/shard_map/ppermute | solution.py:522
  95.9 10.4 %copy-start = (bf16[1,448,256]{2,1,0:T(8,128)(2,1)S(1)}, bf16[1,448,256]{2,1,0:T(8,128)(2,1)}, u32[]{:S(2)}) copy-start(bf16[1,448,256]{2,1,0:T(8,128)(2,1)} %refs_6_.3) | copy-start | bytes 688132
Sparse Core Ops, SparseCore 0:
  24.4 53.2 all-gather.2

commit v5 on v4

--- a/solution.py
+++ b/solution.py
@@ -246,10 +246,23 @@
         backs[s][:, feat:] = tail[rows]
 
 
-def grads_kernel(slot_ref, go_ref, hidden_ref, dgate_ref, dup_ref, gate_out, up_out, down_out):
-    gate_out[0] = contract_rows(slot_ref[...], dgate_ref[...]).astype(BF)
-    up_out[0] = contract_rows(slot_ref[...], dup_ref[...]).astype(BF)
-    down_out[0] = contract_rows(go_ref[...], hidden_ref[...]).astype(BF)
+def grads_kernel(
+    steps, slot_ref, go_ref, hidden_ref, dgate_ref, dup_ref,
+    gate_out, up_out, down_out, buffer, sems,
+):
+    tile = buffer.shape[2] // steps
+    work = ((slot_ref, dgate_ref, gate_out), (slot_ref, dup_ref, up_out), (go_ref, hidden_ref, down_out))
+    copies = []
+    for i in range(steps):
+        part = slice(i * tile, (i + 1) * tile)
+        for n, (rows, units, out) in enumerate(work):
+            buffer[n, :, part] = contract_rows(rows[...], units[:, part]).astype(BF)
+            copies.append(
+                pltpu.make_async_copy(buffer.at[n, :, part], out.at[0, :, part], sems.at[n, i])
+            )
+            copies[-1].start()
+    for copy in copies:
+        copy.wait()
 
 
 def back_rows(backs, feat):
@@ -257,26 +270,35 @@
     return rows[:, :feat].astype(BF), rows[:, feat : feat + 1]
 
 
-def plain_kernel(block_ref, w_ref, *refs):
-    outs, acc_ref = refs[:-1], refs[-1]
-    step = pl.program_id(0)
-    groups, cores, feat, tokens = block_ref.shape
+def plain_kernel(steps, block_ref, w_ref, *refs):
+    outs, (acc_ref, block, weights, sems) = refs[:-4], refs[-4:]
+    groups, near, feat, tokens = block.shape
+    cores = near // steps
     ep = lax.axis_index("ep")
-
-    @pl.when(step == 0)
-    def _():
-        acc_ref[...] = jnp.zeros_like(acc_ref)
-
-    columns = []
+    copies = []
+    for q in range(steps):
+        part = slice(q * cores, (q + 1) * cores)
+        rows = slice(q * cores * feat, (q + 1) * cores * feat)
+        copies.append(
+            (
+                pltpu.make_async_copy(block_ref.at[:, part], block.at[:, part], sems.at[0, q]),
+                pltpu.make_async_copy(w_ref.at[rows, :], weights.at[rows, :], sems.at[1, q]),
+            )
+        )
+        for copy in copies[-1]:
+            copy.start()
+    for q in range(steps):
+        for copy in copies[q]:
+            copy.wait()
+        columns = []
+        for shift in range(groups):
+            g = lax.rem(ep + shift, groups)
+            columns.append(jnp.concatenate([block[g, q * cores + c] for c in range(cores)], axis=0))
+        rows = slice(q * cores * feat, (q + 1) * cores * feat)
+        part = contract_rows(jnp.concatenate(columns, axis=1), weights[rows, :])
+        acc_ref[...] = part if q == 0 else acc_ref[...] + part
     for shift in range(groups):
-        g = lax.rem(ep + shift, groups)
-        columns.append(jnp.concatenate([block_ref[g, c] for c in range(cores)], axis=0))
-    acc_ref[...] += contract_rows(jnp.concatenate(columns, axis=1), w_ref[...])
-
-    @pl.when(step == pl.num_programs(0) - 1)
-    def _():
-        for shift in range(groups):
-            outs[shift][...] = acc_ref[shift * tokens : (shift + 1) * tokens, :].astype(BF)
+        outs[shift][...] = acc_ref[shift * tokens : (shift + 1) * tokens, :].astype(BF)
 
 
 def fixed_kernel(delta_ref, w_ref, *refs):
@@ -306,11 +328,16 @@
         outs[shift][...] = jnp.concatenate(pieces, axis=0).astype(BF)
 
 
-def weight_kernel(block_ref, delta_ref, ctx_ref, out_ref):
-    groups, cores, feat, tokens = block_ref.shape
-    experts, _, _, rows, _ = delta_ref.shape
+def weight_kernel(block_ref, delta_ref, ctx_ref, out_ref, block, result, sems):
+    groups, near, feat, tokens = block.shape
+    experts, steps, cores, rows, _ = delta_ref.shape
     capacity = rows // groups
     ep = lax.axis_index("ep")
+    arrive, leave = [], []
+    for q in range(steps):
+        part = slice(q * cores, (q + 1) * cores)
+        arrive.append(pltpu.make_async_copy(block_ref.at[:, part], block.at[:, part], sems.at[0, q]))
+        arrive[-1].start()
     columns = experts * rows
     row = row_ids((columns, 1))
     group_of = lax.rem(row // rows - lax.rem(row // capacity, groups) + groups, groups)
@@ -320,12 +347,20 @@
     hot = jnp.concatenate(
         [one_hot(jnp.where(group_of == g, pos, -1.0), tokens) for g in order], axis=1
     )
-    blocks = []
-    for c in range(cores):
-        delta = jnp.concatenate([delta_ref[e, 0, c] for e in range(experts)], axis=0)[:, :feat]
-        plain = jnp.concatenate([block_ref[g, c] for g in order], axis=1)
-        blocks.append((plain.astype(F32) + contract_rows(delta, hot)).astype(BF))
-    out_ref[...] = mm(jnp.concatenate(blocks, axis=0), ctx_ref[...]).astype(BF)
+    for q in range(steps):
+        arrive[q].wait()
+        blocks = []
+        for c in range(cores):
+            delta = [delta_ref[e, q, c] for e in range(experts)]
+            delta = jnp.concatenate(delta, axis=0)[:, :feat]
+            plain = jnp.concatenate([block[g, q * cores + c] for g in order], axis=1)
+            blocks.append((plain.astype(F32) + contract_rows(delta, hot)).astype(BF))
+        part = slice(q * cores * feat, (q + 1) * cores * feat)
+        result[part, :] = mm(jnp.concatenate(blocks, axis=0), ctx_ref[...]).astype(BF)
+        leave.append(pltpu.make_async_copy(result.at[part, :], out_ref.at[part, :], sems.at[1, q]))
+        leave[-1].start()
+    for copy in leave:
+        copy.wait()
 
 
 def context_kernel(groups, *refs):
@@ -474,13 +509,15 @@
     spread = lax.ppermute(delta, ("tp", "ep"), route)
     backs = [backs[0]] + [lax.ppermute(backs[s], "ep", behind[s]) for s in range(1, ep_count)]
     grads = call(
-        grads_kernel,
+        functools.partial(grads_kernel, steps),
         [shape_of((1, feat, hidden_units))] * 3,
         [slot_in, rows_go, hidden, d_gate, d_up],
-        [pl.BlockSpec((rows, feat), lambda i: (0, 0))] * 2
-        + [pl.BlockSpec((rows, tile // 2), lambda i: (0, i))] * 3,
-        [pl.BlockSpec((1, feat, tile // 2), lambda i: (0, 0, i))] * 3,
-        grid=(2 * steps,),
+        [VMEM] * 5,
+        [HBM] * 3,
+        scratch=[
+            pltpu.VMEM((3, feat, hidden_units), BF),
+            pltpu.SemaphoreType.DMA((3, steps)),
+        ],
         flops=6 * rows * feat * hidden_units,
     )
     spread, grads = lax.optimization_barrier((spread, grads))
@@ -489,18 +526,19 @@
     spread = spread.reshape(experts, near // 2, 2, rows, lanes)
 
     quarters = near // 2
-    out_block = pl.BlockSpec((groups, 2, feat, tokens), lambda q: (0, q, 0, 0))
-    w_block = pl.BlockSpec((2 * feat, atts), lambda q: (q, 0))
     plain = call(
-        plain_kernel,
+        functools.partial(plain_kernel, quarters),
         [shape_of((tokens, atts))] * groups,
         [block, w_out],
-        [out_block, w_block],
-        [pl.BlockSpec((tokens, atts), lambda q: (0, 0))] * groups,
-        grid=(quarters,),
-        scratch=[pltpu.VMEM((groups * tokens, atts), F32)],
+        [HBM] * 2,
+        [VMEM] * groups,
+        scratch=[
+            pltpu.VMEM((groups * tokens, atts), F32),
+            pltpu.VMEM(block.shape, BF),
+            pltpu.VMEM(w_out.shape, BF),
+            pltpu.SemaphoreType.DMA((2, quarters)),
+        ],
         flops=2 * groups * tokens * near * feat * atts,
-        limit=52,
     )
     spread, plain = lax.optimization_barrier((spread, plain))
     plains = [plain[0]] + [lax.ppermute(plain[s], "ep", ahead[s]) for s in range(1, ep_count)]
@@ -523,16 +561,15 @@
     (w_out_grad,) = call(
         weight_kernel,
         [shape_of((near * feat, atts))],
-        [block, spread.reshape(experts, near, 1, rows, lanes), ctx_all],
-        [
-            pl.BlockSpec((groups, 1, feat, tokens), lambda j: (0, j, 0, 0)),
-            pl.BlockSpec((experts, 1, 1, rows, lanes), lambda j: (0, j, 0, 0, 0)),
-            pl.BlockSpec(ctx_all.shape, lambda j: (0, 0)),
+        [block, spread, ctx_all],
+        [HBM, VMEM, VMEM],
+        [HBM],
+        scratch=[
+            pltpu.VMEM(block.shape, BF),
+            pltpu.VMEM((near * feat, atts), BF),
+            pltpu.SemaphoreType.DMA((2, quarters)),
         ],
-        [pl.BlockSpec((feat, atts), lambda j: (j, 0))],
-        grid=(near,),
         flops=2 * groups * tokens * near * feat * atts,
-        limit=52,
     )
     resid, ctx_grad = call(
         functools.partial(context_kernel, groups),

time: 115 us -> 111 us (0.965)
  Pallas kernels: 37.7 us -> 31.9 us
  waiting for transfers between devices: 26.5 us -> 28.3 us
    pallas_call x9, Pallas kernels: 37.7 us -> 31.9 us  [call(): pl.pallas_call(kernel, out_shape=tuple(outs), in_specs=in_specs, out_spec...]
  transfers between devices with their start and end apart: 11 -> 11, of which waited for: 5 -> 8; matrix products, arithmetic and copies ran while one was open for 1% -> 1% of each run, Pallas kernels for 32% -> 28%
where the time goes in v5:
time: 111 us
  starting transfers between devices  33.8 us (30%)
  Pallas kernels  31.9 us (29%)
  waiting for transfers between devices  28.3 us (25%)
  between operations  14.2 us (13%)
  local copies, waits for them, and re-layouts  2.4 us (2%)
    pallas_call x9, Pallas kernels, call(): pl.pallas_call(kernel, out_shape=tuple(outs), in_specs=in_specs, out_spec...  31.9 us
    all_to_all x1, waiting for transfers between devices, shards(): sums = lax.all_to_all(sums, 'tp', split_axis=0, concat_axis=0, tiled=True)  12.1 us
    all_to_all x1, starting transfers between devices, shards(): lax.all_to_all(spread, 'tp', split_axis=0, concat_axis=0, tiled=True)  11.4 us
    ppermute x1, waiting for transfers between devices, shards(): lax.ppermute(ctx_own, 'ep', ahead[s])  8.57 us
    all_to_all x1, starting transfers between devices, shards(): sums = lax.all_to_all(sums, 'tp', split_axis=0, concat_axis=0, tiled=True)  7.1 us
    ppermute x1, starting transfers between devices, shards(): lax.ppermute(sends[s], 'ep', ahead[s])  5.82 us
    all_to_all x1, starting transfers between devices, shards(): acts = lax.all_to_all(acts, 'tp', split_axis=0, concat_axis=0, tiled=True)  4.49 us
    all_to_all x1, waiting for transfers between devices, shards(): lax.all_to_all(spread, 'tp', split_axis=0, concat_axis=0, tiled=True)  3.14 us
  transfers between devices with their start and end apart: 11, of which 8 were waited for; matrix products, arithmetic and copies ran while one was open for 1% of the time, Pallas kernels for 28%

profile of v5, /device:TPU:0, one launch (start us, length us, event | category | flops | bytes accessed | tf_op | source)
XLA Modules:
  0.0 110.6 jit_solution(6271264989682602551)
XLA Ops:
  7.2 0.0 all-gather.3.cloned.1.call-start
  7.2 1.6 %collective-permute-start.1 = (bf16[448,256]{1,0:T(8,128)(2,1)}, bf16[448,256]{1,0:T(8,128)(2,1)S(1)}, u32[]{:S(2)}, u32[]{:S(2)}) collective-permute-start(bf16[448,256]{1,0:T(8,128)(2,1)} %bitcast.8), channel_id=1, source_target_pairs={{0,0},{1,16},{2,2},{3,18},{4,4},{5,20},{6,6},{7,22},{8,8},{9,24},{... | collective-permute-start | bytes 688136 | tf_op jit(solution)/shard_map/ppermute | solution.py:426
  8.8 2.0 %shard_map.154 = (bf16[32,512]{1,0:T(8,128)(2,1)}, bf16[32,512]{1,0:T(8,128)(2,1)}) custom-call(s32[1,2,8]{2,1,0:T(2,128)} %token_ref.1, s32[1,2]{1,0:T(1,128)} %count_ref.1, f32[1,2,8]{2,1,0:T(2,128)} %gate_ref.1, bf16[1,448,256]{2,1,0:T(8,128)(2,1)} %resid_ref.1, bf16[1,448,256]{2,1,0:T(8,128)(2,1)} %refs_6_.3, f32[1,448]{1,0:T(1,128)} %bitcast.9), custom_call_target="tpu_custom_call" | custom-call | flops 7340032 | bytes 526216 | tf_op jit(solution)/shard_map/pallas_call | solution.py:56
  10.8 5.8 %collective-permute-start = (bf16[32,512]{1,0:T(8,128)(2,1)}, bf16[32,512]{1,0:T(8,128)(2,1)S(1)}, u32[]{:S(2)}, u32[]{:S(2)}) collective-permute-start(bf16[32,512]{1,0:T(8,128)(2,1)} %get-tuple-element.44), channel_id=1, source_target_pairs={{0,1},{1,0},{2,3},{3,2},{4,5},{5,4},{6,7},{7,6},{8,9},{9,8},{10,11... | collective-permute-start | bytes 98312 | tf_op jit(solution)/shard_map/ppermute | solution.py:420
  16.6 2.1 %collective-permute-done.refs_1_ = bf16[32,512]{1,0:T(8,128)(2,1)S(1)} collective-permute-done((bf16[32,512]{1,0:T(8,128)(2,1)}, bf16[32,512]{1,0:T(8,128)(2,1)S(1)}, u32[]{:S(2)}, u32[]{:S(2)}) %collective-permute-start) | collective-permute-done | bytes 32800 | tf_op jit(solution)/shard_map/ppermute | solution.py:420
  18.7 0.0 copy-start.1
  18.7 0.8 copy-done.1
  19.5 0.0 copy-start.4
  19.5 4.0 %shard_map.155 = bf16[16,16,512]{2,1,0:T(8,128)(2,1)} custom-call(bf16[32,512]{1,0:T(8,128)(2,1)S(1)} %copy-done.1, bf16[32,512]{1,0:T(8,128)(2,1)S(1)} %collective-permute-done.refs_1_, bf16[1,448,2048]{2,1,0:T(8,128)(2,1)} %refs_5_.1, bf16[1,448,2048]{2,1,0:T(8,128)(2,1)} %refs_6_.2, bf16[1,448,2048]{2,1,0:T(8,128)(2,1)} %refs_4_.1), custom_call_target="tpu_custom_call" | custom-call | flops 88080384 | bytes 5832704 | tf_op jit(solution)/shard_map/pallas_call | solution.py:56
  23.5 0.0 collective-permute-done.1
  23.6 0.0 copy-start.5
  23.6 0.7 copy-done.5
  24.2 0.0 all-gather.3.cloned.1.call-update
  24.3 7.1 %all-to-all-start = ((bf16[16,16,512]{2,1,0:T(8,128)(2,1)}), bf16[16,16,512]{2,1,0:T(8,128)(2,1)S(1)}, u32[]{:S(2)}, u32[]{:S(2)}) async-start(bf16[16,16,512]{2,1,0:T(8,128)(2,1)} %shard_map.155), calls=%async_computation | async-start | bytes 524288 | tf_op jit(solution)/shard_map/all_to_all | solution.py:455
  31.4 0.0 copy-done.4
  31.4 0.0 copy-start.2
  31.4 0.0 copy-start.3
  31.4 0.2 copy.17
  31.6 12.1 %all-to-all-done.sums_ref = bf16[16,16,512]{2,1,0:T(8,128)(2,1)S(1)} async-done(((bf16[16,16,512]{2,1,0:T(8,128)(2,1)}), bf16[16,16,512]{2,1,0:T(8,128)(2,1)S(1)}, u32[]{:S(2)}, u32[]{:S(2)}) %all-to-all-start) | async-done | bytes 262176 | tf_op jit(solution)/shard_map/all_to_all | solution.py:455
  43.8 1.0 shard_map.156
  44.8 0.0 collective-permute-start.2
  44.8 4.5 %all-to-all-start.1 = ((bf16[16,16,512]{2,1,0:T(8,128)(2,1)}), bf16[16,16,512]{2,1,0:T(8,128)(2,1)S(1)}, u32[]{:S(2)}, u32[]{:S(2)}) async-start(bf16[16,16,512]{2,1,0:T(8,128)(2,1)} %get-tuple-element.47), calls=%async_computation.1 | async-start | bytes 524288 | tf_op jit(solution)/shard_map/all_to_all | solution.py:469
  49.3 8.6 %collective-permute-done.2 = bf16[256,1024]{1,0:T(8,128)(2,1)S(1)} collective-permute-done((bf16[256,1024]{1,0:T(8,128)(2,1)S(1)}, bf16[256,1024]{1,0:T(8,128)(2,1)S(1)}, u32[]{:S(2)}, u32[]{:S(2)}) %collective-permute-start.2) | collective-permute-done | bytes 524320 | tf_op jit(solution)/shard_map/ppermute | solution.py:472
  57.8 0.1 pad_maximum_fusion.ctx_ref
  57.9 1.4 %all-to-all-done.1.refs_2_ = bf16[16,16,512]{2,1,0:T(8,128)(2,1)S(1)} async-done(((bf16[16,16,512]{2,1,0:T(8,128)(2,1)}), bf16[16,16,512]{2,1,0:T(8,128)(2,1)S(1)}, u32[]{:S(2)}, u32[]{:S(2)}) %all-to-all-start.1) | async-done | bytes 262176 | tf_op jit(solution)/shard_map/all_to_all | solution.py:469
  59.3 0.0 copy-done.2
  59.3 0.0 copy-done.3
  59.3 2.5 %shard_map.157 = (bf16[16,2048]{1,0:T(8,128)(2,1)S(1)}, bf16[16,2048]{1,0:T(8,128)(2,1)S(1)}, bf16[16,2048]{1,0:T(8,128)(2,1)S(1)}, bf16[16,448]{1,0:T(8,128)(2,...) custom-call(bf16[32,512]{1,0:T(8,128)(2,1)S(1)} %copy-done.2, ...), custom_call_target="tpu_custom_call" | custom-call | flops 58720256 | bytes 4282112 | tf_op jit(solution)/shard_map/pallas_call | solution.py:56
  61.9 0.7 collective-permute-start.4
  62.5 2.8 %shard_map.158 = (bf16[1,448,2048]{2,1,0:T(8,128)(2,1)}, bf16[1,448,2048]{2,1,0:T(8,128)(2,1)}, bf16[1,448,2048]{2,1,0:T(8,128)(2,1)}) custom-call(bf16[16,448]{1,0:T(8,128)(2,1)S(1)} %get-tuple-element.54.slot_ref, bf16[16,448]{1,0:T(8,128)(2,1)S(1)} %get-tuple-element.55.go_ref, bf16[16,2048]{1,0:T(8,128)(2,1)S(1)} %get-tuple-element.56.hidden_ref, ...), custom_call_target="tpu_custom_call" | custom-call | flops 88080384 | bytes 5730304 | tf_op jit(solution)/shard_map/pallas_call | solution.py:56
  65.4 0.0 collective-permute-done.4
  65.4 0.7 broadcast_in_dim.5
  66.1 11.4 %all-to-all-start.2 = ((bf16[16,16,512]{2,1,0:T(8,128)(2,1)}), bf16[16,16,512]{2,1,0:T(8,128)(2,1)S(1)}, u32[]{:S(2)}, u32[]{:S(2)}) async-start(bf16[16,16,512]{2,1,0:T(8,128)(2,1)} %broadcast_in_dim.5), calls=%async_computation.2 | async-start | bytes 524288 | tf_op jit(solution)/shard_map/all_to_all | solution.py:525
  77.5 0.3 all-gather.3.cloned.1.call-done
  77.8 6.6 %shard_map.159 = (bf16[256,1024]{1,0:T(8,128)(2,1)S(1)}, bf16[256,1024]{1,0:T(8,128)(2,1)S(1)}) custom-call(bf16[2,8,448,256]{3,2,1,0:T(8,128)(2,1)} %bitcast.13, bf16[3584,1024]{1,0:T(8,128)(2,1)} %w_ref.3), custom_call_target="tpu_custom_call" | custom-call | flops 3758096384 | bytes 12058624 | tf_op jit(solution)/shard_map/pallas_call | solution.py:56
  84.4 3.1 %all-to-all-done.2 = bf16[16,16,512]{2,1,0:T(8,128)(2,1)S(1)} async-done(((bf16[16,16,512]{2,1,0:T(8,128)(2,1)}), bf16[16,16,512]{2,1,0:T(8,128)(2,1)S(1)}, u32[]{:S(2)}, u32[]{:S(2)}) %all-to-all-start.2) | async-done | bytes 262176 | tf_op jit(solution)/shard_map/all_to_all | solution.py:525
  87.5 0.6 collective-permute-start.5
  88.1 1.4 %collective-permute-start.3 = (f32[8,512]{1,0:T(8,128)S(1)}, f32[8,512]{1,0:T(8,128)S(1)}, u32[]{:S(2)}, u32[]{:S(2)}) collective-permute-start(f32[8,512]{1,0:T(8,128)S(1)} %get-tuple-element.52), channel_id=1, source_target_pairs={{0,1},{1,0},{2,3},{3,2},{4,5},{5,4},{6,7},{7,6},{8,9},{9,8},{10,11... | collective-permute-start | bytes 49160 | tf_op jit(solution)/shard_map/ppermute | solution.py:510
  89.5 3.4 %shard_map.160 = (bf16[16,1024]{1,0:T(8,128)(2,1)S(1)}, bf16[16,1024]{1,0:T(8,128)(2,1)S(1)}) custom-call(bf16[2,4,2,16,512]{4,3,2,1,0:T(8,128)(2,1)S(1)} %bitcast.6, bf16[3584,1024]{1,0:T(8,128)(2,1)} %w_ref.3), custom_call_target="tpu_custom_call" | custom-call | flops 234881024 | bytes 7667712 | tf_op jit(solution)/shard_map/pallas_call | solution.py:56
  93.0 0.0 copy-start
  93.0 0.7 collective-permute-start.6
  93.7 8.0 %shard_map.162 = bf16[3584,1024]{1,0:T(8,128)(2,1)} custom-call(bf16[2,8,448,256]{3,2,1,0:T(8,128)(2,1)} %bitcast.14, bf16[2,4,2,16,512]{4,3,2,1,0:T(8,128)(2,1)S(1)} %bitcast.7, bf16[512,1024]{1,0:T(8,128)(2,1)S(1)} %pad_maximum_fusion.ctx_ref), custom_call_target="tpu_custom_call" | custom-call | flops 3758096384 | bytes 12320768 | tf_op jit(solution)/shard_map/pallas_call | solution.py:56
  101.6 0.3 collective-permute-done.3.refs_1_
  101.9 0.4 collective-permute-done.6.refs_5_
  102.3 0.0 collective-permute-done.5.refs_3_
  102.3 0.0 copy-done
  102.3 1.5 %shard_map.161 = (bf16[1,448,256]{2,1,0:T(8,128)(2,1)}, bf16[1,1024,256]{2,1,0:T(8,128)(2,1)}) custom-call(f32[8,512]{1,0:T(8,128)S(1)} %get-tuple-element.51.refs_0_, f32[8,512]{1,0:T(8,128)S(1)} %collective-permute-done.3.refs_1_, bf16[256,1024]{1,0:T(8,128)(2,1)S(1)} %get-tuple-element.66.refs_2_, bf16[256,1024]{1,0:T(8,128)(2,1)S(1)} %collective-permute-done.5.refs_3_, ...), custom_call_target="tpu_custom_call" | custom-call | flops 12058624 | bytes 2129920 | tf_op jit(solution)/shard_map/pallas_call | solution.py:56
Async XLA Ops:
  7.2 70.6 %all-gather.3.cloned.1.call-start = ((), (), s32[]{:S(2)}) async-start(), calls=%async_computation.3 | async-start | bytes 3899392 | tf_op jit(solution)/shard_map/all_gather | solution.py:454
  7.2 16.3 %collective-permute-start.1 = (bf16[448,256]{1,0:T(8,128)(2,1)}, bf16[448,256]{1,0:T(8,128)(2,1)S(1)}, u32[]{:S(2)}, u32[]{:S(2)}) collective-permute-start(bf16[448,256]{1,0:T(8,128)(2,1)} %bitcast.8), channel_id=1, source_target_pairs={{0,0},{1,16},{2,2},{3,18},{4,4},{5,20},{6,6},{7,22},{8,8},{9,24},{... | collective-permute-start | bytes 688136 | tf_op jit(solution)/shard_map/ppermute | solution.py:426
  10.8 7.9 %collective-permute-start = (bf16[32,512]{1,0:T(8,128)(2,1)}, bf16[32,512]{1,0:T(8,128)(2,1)S(1)}, u32[]{:S(2)}, u32[]{:S(2)}) collective-permute-start(bf16[32,512]{1,0:T(8,128)(2,1)} %get-tuple-element.44), channel_id=1, source_target_pairs={{0,1},{1,0},{2,3},{3,2},{4,5},{5,4},{6,7},{7,6},{8,9},{9,8},{10,11... | collective-permute-start | bytes 98312 | tf_op jit(solution)/shard_map/ppermute | solution.py:420
  18.7 0.8 copy-start.1
  19.5 11.9 %copy-start.4 = (bf16[1,1024,256]{2,1,0:T(8,128)(2,1)S(1)}, bf16[1,1024,256]{2,1,0:T(8,128)(2,1)}, u32[]{:S(2)}) copy-start(bf16[1,1024,256]{2,1,0:T(8,128)(2,1)} %param.14) | copy-start | bytes 1572868
  23.6 0.7 copy-start.5
  24.3 19.5 %all-to-all-start = ((bf16[16,16,512]{2,1,0:T(8,128)(2,1)}), bf16[16,16,512]{2,1,0:T(8,128)(2,1)S(1)}, u32[]{:S(2)}, u32[]{:S(2)}) async-start(bf16[16,16,512]{2,1,0:T(8,128)(2,1)} %shard_map.155), calls=%async_computation | async-start | bytes 524288 | tf_op jit(solution)/shard_map/all_to_all | solution.py:455
  31.4 27.9 %copy-start.2 = (bf16[32,512]{1,0:T(8,128)(2,1)S(1)}, bf16[32,512]{1,0:T(8,128)(2,1)}, u32[]{:S(2)}) copy-start(bf16[32,512]{1,0:T(8,128)(2,1)} %get-tuple-element.43.refs_0_) | copy-start | bytes 98308
  31.4 27.9 %copy-start.3 = (f32[448]{0:T(512)S(1)}, f32[448]{0:T(512)}, u32[]{:S(2)}) copy-start(f32[448]{0:T(512)} %param.13) | copy-start | bytes 5380
  44.8 13.1 %collective-permute-start.2 = (bf16[256,1024]{1,0:T(8,128)(2,1)S(1)}, bf16[256,1024]{1,0:T(8,128)(2,1)S(1)}, u32[]{:S(2)}, u32[]{:S(2)}) collective-permute-start(bf16[256,1024]{1,0:T(8,128)(2,1)S(1)} %bitcast.11), channel_id=1, source_target_pairs={{0,1},{1,0},{2,3},{3,2},{4,5},{5,4},{6,7},{7,6},{8,9},{9,8},{10,11... | collective-permute-start | bytes 1572872 | tf_op jit(solution)/shard_map/ppermute | solution.py:472
  44.8 14.6 %all-to-all-start.1 = ((bf16[16,16,512]{2,1,0:T(8,128)(2,1)}), bf16[16,16,512]{2,1,0:T(8,128)(2,1)S(1)}, u32[]{:S(2)}, u32[]{:S(2)}) async-start(bf16[16,16,512]{2,1,0:T(8,128)(2,1)} %get-tuple-element.47), calls=%async_computation.1 | async-start | bytes 524288 | tf_op jit(solution)/shard_map/all_to_all | solution.py:469
  61.9 3.5 %collective-permute-start.4 = (bf16[16,512]{1,0:T(8,128)(2,1)S(1)}, bf16[16,512]{1,0:T(8,128)(2,1)S(1)}, u32[]{:S(2)}, u32[]{:S(2)}) collective-permute-start(bf16[16,512]{1,0:T(8,128)(2,1)S(1)} %get-tuple-element.53), channel_id=1, source_target_pairs={{0,0},{1,16},{2,2},{3,18},{4,4},{5,20},{6,6},{7,22},{8,8},{9,24},{... | collective-permute-start | bytes 49160 | tf_op jit(solution)/shard_map/ppermute | solution.py:509
  66.1 21.4 %all-to-all-start.2 = ((bf16[16,16,512]{2,1,0:T(8,128)(2,1)}), bf16[16,16,512]{2,1,0:T(8,128)(2,1)S(1)}, u32[]{:S(2)}, u32[]{:S(2)}) async-start(bf16[16,16,512]{2,1,0:T(8,128)(2,1)} %broadcast_in_dim.5), calls=%async_computation.2 | async-start | bytes 524288 | tf_op jit(solution)/shard_map/all_to_all | solution.py:525
  87.5 14.7 %collective-permute-start.5 = (bf16[256,1024]{1,0:T(8,128)(2,1)S(1)}, bf16[256,1024]{1,0:T(8,128)(2,1)S(1)}, u32[]{:S(2)}, u32[]{:S(2)}) collective-permute-start(bf16[256,1024]{1,0:T(8,128)(2,1)S(1)} %get-tuple-element.67), channel_id=1, source_target_pairs={{0,1},{1,0},{2,3},{3,2},{4,5},{5,4},{6,7},{7,6},{8,9},{9,8},{10,11... | collective-permute-start | bytes 1572872 | tf_op jit(solution)/shard_map/ppermute | solution.py:544
  88.1 13.8 %collective-permute-start.3 = (f32[8,512]{1,0:T(8,128)S(1)}, f32[8,512]{1,0:T(8,128)S(1)}, u32[]{:S(2)}, u32[]{:S(2)}) collective-permute-start(f32[8,512]{1,0:T(8,128)S(1)} %get-tuple-element.52), channel_id=1, source_target_pairs={{0,1},{1,0},{2,3},{3,2},{4,5},{5,4},{6,7},{7,6},{8,9},{9,8},{10,11... | collective-permute-start | bytes 49160 | tf_op jit(solution)/shard_map/ppermute | solution.py:510
  93.0 9.3 %copy-start = (bf16[1,448,256]{2,1,0:T(8,128)(2,1)S(1)}, bf16[1,448,256]{2,1,0:T(8,128)(2,1)}, u32[]{:S(2)}) copy-start(bf16[1,448,256]{2,1,0:T(8,128)(2,1)} %refs_6_.3) | copy-start | bytes 688132
  93.0 9.2 %collective-permute-start.6 = (bf16[16,1024]{1,0:T(8,128)(2,1)S(1)}, bf16[16,1024]{1,0:T(8,128)(2,1)S(1)}, u32[]{:S(2)}, u32[]{:S(2)}) collective-permute-start(bf16[16,1024]{1,0:T(8,128)(2,1)S(1)} %get-tuple-element.72), channel_id=1, source_target_pairs={{0,1},{1,0},{2,3},{3,2},{4,5},{5,4},{6,7},{7,6},{8,9},{9,8},{10,11... | collective-permute-start | bytes 98312 | tf_op jit(solution)/shard_map/ppermute | solution.py:560
Sparse Core Ops, SparseCore 0:
  24.4 53.3 all-gather.2
